TPU v7x, 512 devices: a whole 4x4x16 slice. The times are simulated.
512 devices in a mesh: vocab: 64 (over z, x), pass: 8 (over y, core).
Axes of the slice: x: 4, y: 4, z: 16, core: 2. Of those that a mesh axis runs over, the one named last changes fastest.
Arguments:
- hidden: bfloat16 [768, 1024], P('pass'), as said below
- weight: bfloat16 [1024, 196608], P(None, ('vocab', 'pass')), may hold values from -0.1875 to 0.1875
- bias: float32 [196608], P(('vocab', 'pass')), may hold values from -6 to 6
- token_ids: int32 [24, 32], replicated, may hold values from 1 to 250001, as said below
- passages: bfloat16 [1024, 196608], P('pass', 'vocab'), as said below
- positive: int32 [24], replicated, may hold values from 0 to 1023
- selected: int32 [24, 196608], P(None, ('vocab', 'pass')), may hold values from 0 to 31, as said below
Outputs:
- mean_loss: float32 [], replicated
- grad_hidden: bfloat16 [768, 1024], P('vocab', 'pass')
- grad_weight: float32 [1024, 196608], P(None, ('vocab', 'pass'))
- grad_bias: float32 [196608], P(('vocab', 'pass'))
Inputs may be any that keep to these rules, and one draw needn't show every extreme that they name: `token_ids`: each query has 8 to 32 real tokens, first, then padding id 1; other ids are at least 5. selected[q, v] names a real, not padding, position of query q. `passages`: entries lie within -0.03 to 0.03. `hidden`: entries lie within -6 to 6.
All inputs are finite; a program needn't handle non-finite values.
Results may differ from a plain program's by a relative error of at most 0.013.
Values may be sent and summed in bfloat16 or wider, within the bound.
A program may use at most 64 MiB of HBM per device.

v0:
```python
import jax
import jax.numpy as jnp
from jax import lax
from jax.sharding import PartitionSpec as P

loss_scale = 4096.0


def local(hidden, weight, bias, token_ids, passages, positive, selected):
    num_queries, query_len = token_ids.shape
    gathered = lax.all_gather(hidden, "pass", axis=0, tiled=True)
    logits = jnp.dot(gathered, weight, preferred_element_type=jnp.float32) + bias[None, :]
    valid_mask = (token_ids != 1).astype(jnp.float32)
    activation = (
        jnp.log1p(jax.nn.softplus(logits)).reshape(num_queries, query_len, -1)
        * valid_mask[:, :, None]
    )
    pooled = jnp.max(activation, axis=1).astype(jnp.bfloat16)
    group_terms = lax.all_gather(pooled, "pass", axis=1, tiled=True)
    partial_value = lax.dot_general(
        group_terms, passages, (((1,), (1,)), ((), ())), preferred_element_type=jnp.float32
    )
    scores = lax.psum(partial_value, "vocab")
    block_cols = scores.shape[1]
    first_col = lax.axis_index("pass") * block_cols
    column = first_col + jnp.arange(block_cols, dtype=jnp.int32)
    onehot = (column[None, :] == positive[:, None]).astype(jnp.float32)
    peak_score = lax.pmax(jnp.max(scores, axis=1), "pass")
    exp_terms = jnp.exp(scores - peak_score[:, None])
    total_exp, pos_score = lax.psum(
        (jnp.sum(exp_terms, axis=1), jnp.sum(scores * onehot, axis=1)), "pass"
    )
    log_total = peak_score + jnp.log(total_exp)
    mean_loss = jnp.mean(log_total - pos_score)
    softmax_probs = jnp.exp(scores - log_total[:, None])
    score_grad = ((softmax_probs - onehot) * (loss_scale / num_queries)).astype(jnp.bfloat16)
    term_part = jnp.dot(score_grad, passages, preferred_element_type=jnp.float32)
    term_grad = lax.psum_scatter(term_part, "pass", scatter_dimension=1, tiled=True)
    slopes = (jax.nn.sigmoid(logits) / (1.0 + jax.nn.softplus(logits))).reshape(
        num_queries, query_len, -1
    )
    positions = jnp.arange(query_len, dtype=jnp.int32)
    chosen = positions[None, :, None] == selected[:, None, :]
    logit_grad = jnp.where(chosen, slopes * term_grad[:, None, :], jnp.zeros_like(slopes)).reshape(
        num_queries * query_len, -1
    )
    grad_bias = jnp.sum(logit_grad, axis=0)
    logit_half = logit_grad.astype(jnp.bfloat16)
    grad_weight = lax.dot_general(
        gathered, logit_half, (((0,), (0,)), ((), ())), preferred_element_type=jnp.float32
    )
    partial_hidden = lax.dot_general(
        logit_half, weight, (((1,), (1,)), ((), ())), preferred_element_type=jnp.float32
    )
    vocab_summed = lax.psum_scatter(partial_hidden, "vocab", scatter_dimension=0, tiled=True)
    hidden_total = lax.psum_scatter(vocab_summed, "pass", scatter_dimension=1, tiled=True)
    return (mean_loss, hidden_total.astype(jnp.bfloat16), grad_weight, grad_bias)


def solution(mesh):
    in_specs = (
        P("pass", None),
        P(None, ("vocab", "pass")),
        P(("vocab", "pass")),
        P(),
        P("pass", "vocab"),
        P(),
        P(None, ("vocab", "pass")),
    )
    out_specs = (P(), P("vocab", "pass"), P(None, ("vocab", "pass")), P(("vocab", "pass")))
    return jax.shard_map(local, mesh=mesh, in_specs=in_specs, out_specs=out_specs, check_vma=False)
```

profile of v0, /device:TPU:1, one launch (start us, length us, event | category | flops | bytes accessed | tf_op | source)
XLA Modules:
  0.0 681.0 jit_solution(8776346305522341505)
XLA Ops:
  8.7 39.2 %all-gather.2.cloned.1.call-done = bf16[768,1024]{1,0:T(8,128)(2,1)} async-done(((bf16[96,1024]{1,0:T(8,128)(2,1)}), bf16[768,1024]{1,0:T(8,128)(2,1)}) %all-gather.2.cloned.1.call-update) | async-done | bytes 1572880 | tf_op jit(solution)/shard_map/all_gather | solution.py:11
  47.9 3.2 fusion.2
  51.5 12.9 %all_gather.7 = bf16[24,3072]{1,0:T(8,128)(2,1)S(1)} all-gather(bf16[24,384]{1,0:T(8,128)(2,1)S(1)} %multiply_reduce_fusion), channel_id=1, replica_groups=mesh['vocab'=64,'pass'=8] {'pass'}, dimensions={1}, use_global_device_ids=true | all-gather | bytes 165888 | tf_op jit(solution)/shard_map/all_gather | solution.py:19
  64.6 225.3 %psum.21 = f32[24,128]{1,0:T(8,128)S(1)} all-reduce(f32[24,128]{1,0:T(8,128)S(1)} %fusion.19), channel_id=1, replica_groups=mesh['vocab'=64,'pass'=8] {'vocab'}, use_global_device_ids=true, to_apply=%region_1.2 | all-reduce | flops 3072 | bytes 24576 | tf_op jit(solution)/shard_map/psum | solution.py:23
  290.1 66.7 %pmax.7 = f32[24]{0:T(128)S(1)} all-reduce(f32[24]{0:T(128)S(1)} %reduce_max.19), channel_id=1, replica_groups=mesh['vocab'=64,'pass'=8] {'pass'}, use_global_device_ids=true, to_apply=%region_3.4 | all-reduce | flops 24 | bytes 192 | tf_op jit(solution)/shard_map/pmax | solution.py:28
  357.0 12.4 %all-reduce.2 = (f32[24]{0:T(128)S(1)}, f32[24]{0:T(128)S(1)}) all-reduce(f32[24]{0:T(128)S(1)} %get-tuple-element.13, f32[24]{0:T(128)S(1)} %get-tuple-element.12), channel_id=1, replica_groups=mesh['vocab'=64,'pass'=8] {'pass'}, use_global_device_ids=true, to_apply=%region_5.6 | all-reduce | flops 48 | bytes 384 | tf_op jit(solution)/shard_map/psum | solution.py:30
  371.2 29.6 %reduce-scatter.5.cloned.1.call-done = f32[24,384]{1,0:T(8,128)} async-done(((f32[24,3072]{1,0:T(8,128)}), f32[24,384]{1,0:T(8,128)}) %reduce-scatter.5.cloned.1.call-update) | async-done | bytes 36880 | tf_op jit(solution)/shard_map/reduce_scatter | solution.py:38
  400.8 2.4 fusion.17
  403.2 2.7 fusion.4
  405.9 142.2 %fusion = f32[16,1024]{1,0:T(8,128)S(1)} fusion(f32[768,1024]{1,0:T(8,128)} %fusion.4), kind=kCustom, calls=%all-reduce-scatter | all-reduce-scatter fusion | flops 1048577 | bytes 3213312
  548.1 3.7 collective-permute-start.15
  551.8 6.1 collective-permute-start.14
  557.9 1.9 collective-permute-start.13
  559.8 1.3 collective-permute-start.12
  561.1 1.3 collective-permute-start.11
  562.4 7.6 %collective-permute-start.10 = (f32[16,1024]{1,0:T(8,128)S(1)}, f32[16,1024]{1,0:T(8,128)S(1)}, u32[]{:S(2)}, u32[]{:S(2)}) collective-permute-start(f32[16,1024]{1,0:T(8,128)S(1)} %fusion), channel_id=1, source_target_pairs={{0,88},{8,96},{16,104},{24,112},{32,120},{40,128},{48,136},{56,144... | collective-permute-start | bytes 196616
  570.0 6.7 collective-permute-start.9
  576.7 1.9 collective-permute-start.8
  578.7 2.5 collective-permute-start.7
  581.2 2.8 collective-permute-start.6
  584.0 1.6 collective-permute-start.5
  585.7 3.1 collective-permute-start.4
  588.8 2.2 collective-permute-start.3
  591.0 4.4 collective-permute-start.2
  595.4 2.7 collective-permute-start.1
  598.2 2.6 collective-permute-start
  600.8 1.3 dynamic-slice.4
  603.4 3.0 concatenate
  607.0 2.2 convolution_bitcast_fusion
  609.2 1.6 copy.12
  610.8 61.2 %reduce-scatter.7.cloned.1.call-done = f32[12,128]{1,0:T(8,128)} async-done(((f32[12,1024]{1,0:T(8,128)}), f32[12,128]{1,0:T(8,128)}) %reduce-scatter.7.cloned.1.call-update) | async-done | bytes 6160 | tf_op jit(solution)/shard_map/reduce_scatter | solution.py:56
  672.1 1.3 convert_element_type.23
  (42 shorter events, 4.8 us)
Async XLA Ops:
  7.2 40.8 %copy-start = (bf16[1024,384]{1,0:T(8,128)(2,1)S(1)}, bf16[1024,384]{1,0:T(8,128)(2,1)}, u32[]{:S(2)}) copy-start(bf16[1024,384]{1,0:T(8,128)(2,1)} %param.8) | copy-start | bytes 2359300
  7.2 40.7 %all-gather.2.cloned.1.call-start = ((), (), s32[]{:S(2)}) async-start(), calls=%async_computation.2 | async-start | bytes 1769472 | tf_op jit(solution)/shard_map/all_gather | solution.py:11
  7.9 392.9 %reduce-scatter.5.cloned.1.call-start = ((), (), s32[]{:S(2)}) async-start(), calls=%async_computation.3 | async-start | bytes 331776 | tf_op jit(solution)/shard_map/reduce_scatter | solution.py:38
  51.2 13.2 %copy-start.1 = (bf16[128,3072]{1,0:T(8,128)(2,1)S(1)}, bf16[128,3072]{1,0:T(8,128)(2,1)}, u32[]{:S(2)}) copy-start(bf16[128,3072]{1,0:T(8,128)(2,1)} %param.11) | copy-start | bytes 2359300
  51.2 305.6 %copy-start.3 = (s32[24]{0:T(128)S(1)}, s32[24]{0:T(128)}, u32[]{:S(2)}) copy-start(s32[24]{0:T(128)} %param.12) | copy-start | bytes 292
  64.3 336.5 %copy-start.2 = (s32[24,384]{1,0:T(8,128)S(1)}, s32[24,384]{1,0:T(8,128)}, u32[]{:S(2)}) copy-start(s32[24,384]{1,0:T(8,128)} %param.13) | copy-start | bytes 110596
  371.1 301.0 %reduce-scatter.7.cloned.1.call-start = ((), (), s32[]{:S(2)}) async-start(), calls=%async_computation.4 | async-start | bytes 73728 | tf_op jit(solution)/shard_map/reduce_scatter | solution.py:56
  548.1 14.3 %collective-permute-start.15 = (f32[12,1024]{1,0:T(8,128)S(1)}, f32[12,1024]{1,0:T(8,128)S(1)}, u32[]{:S(2)}, u32[]{:S(2)}) collective-permute-start(f32[12,1024]{1,0:T(8,128)S(1)} %slice), channel_id=1, source_target_pairs={{0,128},{8,136},{16,144},{24,152},{32,160},{40,168},{48,176},{56,1... | collective-permute-start | bytes 147464
  551.8 18.2 %collective-permute-start.14 = (f32[16,1024]{1,0:T(8,128)S(1)}, f32[16,1024]{1,0:T(8,128)S(1)}, u32[]{:S(2)}, u32[]{:S(2)}) collective-permute-start(f32[16,1024]{1,0:T(8,128)S(1)} %fusion), channel_id=1, source_target_pairs={{0,120},{8,128},{16,136},{24,144},{32,152},{40,160},{48,168},{56,1... | collective-permute-start | bytes 196616
  557.9 18.8 %collective-permute-start.13 = (f32[16,1024]{1,0:T(8,128)S(1)}, f32[16,1024]{1,0:T(8,128)S(1)}, u32[]{:S(2)}, u32[]{:S(2)}) collective-permute-start(f32[16,1024]{1,0:T(8,128)S(1)} %fusion), channel_id=1, source_target_pairs={{0,112},{8,120},{16,128},{24,136},{32,144},{40,152},{48,160},{56,1... | collective-permute-start | bytes 196616
  559.8 18.9 %collective-permute-start.12 = (f32[16,1024]{1,0:T(8,128)S(1)}, f32[16,1024]{1,0:T(8,128)S(1)}, u32[]{:S(2)}, u32[]{:S(2)}) collective-permute-start(f32[16,1024]{1,0:T(8,128)S(1)} %fusion), channel_id=1, source_target_pairs={{0,104},{8,112},{16,120},{24,128},{32,136},{40,144},{48,152},{56,1... | collective-permute-start | bytes 196616
  561.1 20.1 %collective-permute-start.11 = (f32[16,1024]{1,0:T(8,128)S(1)}, f32[16,1024]{1,0:T(8,128)S(1)}, u32[]{:S(2)}, u32[]{:S(2)}) collective-permute-start(f32[16,1024]{1,0:T(8,128)S(1)} %fusion), channel_id=1, source_target_pairs={{0,96},{8,104},{16,112},{24,120},{32,128},{40,136},{48,144},{56,15... | collective-permute-start | bytes 196616
  562.4 21.6 %collective-permute-start.10 = (f32[16,1024]{1,0:T(8,128)S(1)}, f32[16,1024]{1,0:T(8,128)S(1)}, u32[]{:S(2)}, u32[]{:S(2)}) collective-permute-start(f32[16,1024]{1,0:T(8,128)S(1)} %fusion), channel_id=1, source_target_pairs={{0,88},{8,96},{16,104},{24,112},{32,120},{40,128},{48,136},{56,144... | collective-permute-start | bytes 196616
  570.0 15.6 %collective-permute-start.9 = (f32[16,1024]{1,0:T(8,128)S(1)}, f32[16,1024]{1,0:T(8,128)S(1)}, u32[]{:S(2)}, u32[]{:S(2)}) collective-permute-start(f32[16,1024]{1,0:T(8,128)S(1)} %fusion), channel_id=1, source_target_pairs={{0,80},{8,88},{16,96},{24,104},{32,112},{40,120},{48,128},{56,136}... | collective-permute-start | bytes 196616
  576.7 12.0 %collective-permute-start.8 = (f32[16,1024]{1,0:T(8,128)S(1)}, f32[16,1024]{1,0:T(8,128)S(1)}, u32[]{:S(2)}, u32[]{:S(2)}) collective-permute-start(f32[16,1024]{1,0:T(8,128)S(1)} %fusion), channel_id=1, source_target_pairs={{0,72},{8,80},{16,88},{24,96},{32,104},{40,112},{48,120},{56,128},... | collective-permute-start | bytes 196616
  578.7 12.3 %collective-permute-start.7 = (f32[16,1024]{1,0:T(8,128)S(1)}, f32[16,1024]{1,0:T(8,128)S(1)}, u32[]{:S(2)}, u32[]{:S(2)}) collective-permute-start(f32[16,1024]{1,0:T(8,128)S(1)} %fusion), channel_id=1, source_target_pairs={{0,64},{8,72},{16,80},{24,88},{32,96},{40,104},{48,112},{56,120},{... | collective-permute-start | bytes 196616
  581.2 14.2 %collective-permute-start.6 = (f32[16,1024]{1,0:T(8,128)S(1)}, f32[16,1024]{1,0:T(8,128)S(1)}, u32[]{:S(2)}, u32[]{:S(2)}) collective-permute-start(f32[16,1024]{1,0:T(8,128)S(1)} %fusion), channel_id=1, source_target_pairs={{0,56},{8,64},{16,72},{24,80},{32,88},{40,96},{48,104},{56,112},{6... | collective-permute-start | bytes 196616
  584.0 14.1 %collective-permute-start.5 = (f32[16,1024]{1,0:T(8,128)S(1)}, f32[16,1024]{1,0:T(8,128)S(1)}, u32[]{:S(2)}, u32[]{:S(2)}) collective-permute-start(f32[16,1024]{1,0:T(8,128)S(1)} %fusion), channel_id=1, source_target_pairs={{0,48},{8,56},{16,64},{24,72},{32,80},{40,88},{48,96},{56,104},{64... | collective-permute-start | bytes 196616
  585.7 17.7 %collective-permute-start.4 = (f32[16,1024]{1,0:T(8,128)S(1)}, f32[16,1024]{1,0:T(8,128)S(1)}, u32[]{:S(2)}, u32[]{:S(2)}) collective-permute-start(f32[16,1024]{1,0:T(8,128)S(1)} %fusion), channel_id=1, source_target_pairs={{0,40},{8,48},{16,56},{24,64},{32,72},{40,80},{48,88},{56,96},{64,... | collective-permute-start | bytes 196616
  588.8 14.6 %collective-permute-start.3 = (f32[16,1024]{1,0:T(8,128)S(1)}, f32[16,1024]{1,0:T(8,128)S(1)}, u32[]{:S(2)}, u32[]{:S(2)}) collective-permute-start(f32[16,1024]{1,0:T(8,128)S(1)} %fusion), channel_id=1, source_target_pairs={{0,32},{8,40},{16,48},{24,56},{32,64},{40,72},{48,80},{56,88},{64,... | collective-permute-start | bytes 196616
  591.0 12.3 %collective-permute-start.2 = (f32[16,1024]{1,0:T(8,128)S(1)}, f32[16,1024]{1,0:T(8,128)S(1)}, u32[]{:S(2)}, u32[]{:S(2)}) collective-permute-start(f32[16,1024]{1,0:T(8,128)S(1)} %fusion), channel_id=1, source_target_pairs={{0,24},{8,32},{16,40},{24,48},{32,56},{40,64},{48,72},{56,80},{64,... | collective-permute-start | bytes 196616
  595.4 7.9 %collective-permute-start.1 = (f32[16,1024]{1,0:T(8,128)S(1)}, f32[16,1024]{1,0:T(8,128)S(1)}, u32[]{:S(2)}, u32[]{:S(2)}) collective-permute-start(f32[16,1024]{1,0:T(8,128)S(1)} %fusion), channel_id=1, source_target_pairs={{0,16},{8,24},{16,32},{24,40},{32,48},{40,56},{48,64},{56,72},{64,... | collective-permute-start | bytes 196616
  598.2 5.2 collective-permute-start
Sparse Core Ops, SparseCore 0:
  10.1 37.7 all-gather.1
  371.2 29.5 reduce-scatter.4
  607.1 64.8 reduce-scatter.6
where the time goes:
time: 683 us; the launch traced here: 681 us
  blocking collectives  460 us (67%)
  waiting for transfers between devices  131 us (19%)
  starting transfers between devices  52.5 us (8%)
  between operations  16.5 us (2%)
  matrix products  9.41 us (1%)
    psum x1, blocking collectives, local(): scores = lax.psum(partial_value, 'vocab')  225 us
    unnamed x1, blocking collectives  142 us
    pmax x1, blocking collectives, local(): peak_score = lax.pmax(jnp.max(scores, axis=1), 'pass')  66.7 us
    reduce_scatter x1, waiting for transfers between devices, local(): lax.psum_scatter(vocab_summed, 'pass', scatter_dimension=1, tiled=True)  61.2 us
    unnamed x16, starting transfers between devices  52.4 us
    all_gather x1, waiting for transfers between devices, local(): gathered = lax.all_gather(hidden, 'pass', axis=0, tiled=True)  39.2 us
    reduce_scatter x1, waiting for transfers between devices, local(): lax.psum_scatter(term_part, 'pass', scatter_dimension=1, tiled=True)  29.6 us
  transfers between devices with their start and end apart: 19, of which 3 were waited for; matrix products, arithmetic and copies ran while one was open for 1% of the time, Pallas kernels for 0%

commit v1 on v0

v1 whole, which is shorter than its diff:
```python
import functools

import jax
import jax.numpy as jnp
from jax import lax
from jax.experimental import pallas as pl
from jax.experimental.pallas import tpu as pltpu
from jax.sharding import PartitionSpec as P

loss_scale = 4096.0
NX = 4
NC = 2
PAD = 8
MESH = pl.DeviceIdType.MESH
f32 = jnp.float32
bf16 = jnp.bfloat16


def dot(a, b):
    return jnp.dot(a, b, preferred_element_type=f32)


def dot_nt(a, b):
    return lax.dot_general(a, b, (((1,), (1,)), ((), ())), preferred_element_type=f32)


def iota(shape, axis):
    return lax.broadcasted_iota(jnp.int32, shape, axis)


def kernel(nz, ny, n_queries, hidden, weight, bias, tokens, passages, positive, selected,
           loss_o, gh_o, gw_o, gb_o,
           gath, gath_t, w_v, ws_t, wo_t, pas, perm, maxl, sell, selp, lenp,
           pool, pos_s, pos_r, sc_s, sc_x, zs, zr, fin, st_s, st, u_s, u_r, slope,
           lh, lhp, cs_s, cs_r, own, s1y, s1y_r, s1x, s1x_r, s2x, s2x_r, s2y, s2y_r,
           zf, z2, z2_r, gw_v, send_sems, recv_sems, loc_sems):
    n_pass = ny * NC
    v = lax.axis_index("vocab")
    p = lax.axis_index("pass")
    z, x = lax.div(v, NX), lax.rem(v, NX)
    y, c = lax.div(p, NC), lax.rem(p, NC)
    sib = 1 - c
    voc = w_v.shape[1]
    group = n_queries // NX
    rows = NX * PAD
    hz = nz // 2
    tok = gath.shape[0] * gath.shape[1]
    half = tok // 2
    ro = tok // (nz * NX)
    part = hz * ro
    cols = ny * 128

    def around(value, shift, size):
        return lax.rem(value + (shift + size), size)

    def pass_dev(dy, dc):
        return (v, around(y, dy, ny) * NC + around(c, dc, NC))

    def x_dev(dx):
        return (z * NX + around(x, dx, NX), p)

    def z_dev(dz):
        return (around(z, dz, nz) * NX + x, p)

    pass_peers = [(dy, dc) for dy in range(ny) for dc in range(NC) if dy or dc]
    started = []

    def remote(src, dst, device):
        i = len(started)
        copy = pltpu.make_async_remote_copy(
            src_ref=src, dst_ref=dst, send_sem=send_sems.at[i], recv_sem=recv_sems.at[i],
            device_id=device, device_id_type=MESH,
        )
        copy.start()
        started.append(copy)
        return copy

    local = [pltpu.make_async_copy(hidden, gath.at[p], loc_sems.at[0]),
             pltpu.make_async_copy(weight, w_v, loc_sems.at[1])]
    for j in range(n_pass):
        local.append(pltpu.make_async_copy(
            passages.at[:, pl.ds(j * voc, voc)], pas.at[j], loc_sems.at[2 + j]))
    for copy in local:
        copy.start()

    barrier = pltpu.get_barrier_semaphore()
    peers = ([pass_dev(dy, dc) for dy, dc in pass_peers] + [x_dev(d) for d in range(1, NX)]
             + [z_dev(d) for d in range(1, nz)])
    for device in peers:
        pl.semaphore_signal(barrier, inc=1, device_id=device, device_id_type=MESH)
    pl.semaphore_wait(barrier, len(peers))

    to_y = {}
    for dy in sorted(range(1, ny), key=lambda d: -min(d, ny - d)):
        to_y[dy] = remote(hidden, gath.at[p], pass_dev(dy, 0))
    to_sib = {0: remote(hidden, gath.at[p], pass_dev(0, 1))}

    maxl[...] = jnp.zeros_like(maxl)
    sell[...] = jnp.zeros_like(sell)
    selp[...] = jnp.zeros_like(selp)
    lenp[...] = jnp.zeros_like(lenp)
    zf[...] = jnp.zeros_like(zf)
    lengths = jnp.sum((tokens[...] != 1).astype(f32), axis=1, keepdims=True)
    lengths = jnp.broadcast_to(lengths, (n_queries, voc))
    for g in range(NX):
        selp[g, 0:group, :] = selected[g * group:(g + 1) * group, :]
        lenp[g, 0:group, :] = lengths[g * group:(g + 1) * group, :].astype(jnp.int32)

    def block(yy):
        first = yy * NC
        got = gath[pl.ds(first, NC)].reshape(NC * gath.shape[1], gath.shape[2])
        logits = dot(got, w_v[...])
        qlen = logits.shape[0] // group
        logits = logits.reshape(group, qlen, voc)
        at = iota((group, qlen, voc), 1)
        valid = at < lenp[yy][0:group].reshape(group, 1, voc)
        chosen = at == selp[yy][0:group].reshape(group, 1, voc)
        maxl[yy, 0:group, :] = jnp.max(jnp.where(valid, logits, -jnp.inf), axis=1)
        sell[yy, 0:group, :] = jnp.sum(jnp.where(chosen, logits, 0.0), axis=1)

    def arrive(dy):
        to_y[dy].wait_recv()
        at = around(y, -dy, ny) * NC + c
        to_sib[dy] = remote(gath.at[at], gath.at[at], pass_dev(0, 1))

    local[0].wait()
    local[1].wait()
    to_sib[0].wait_recv()
    block(y)
    order = sorted(range(1, ny), key=lambda d: min(d, ny - d))
    for i, dy in enumerate(order):
        if i == 0:
            arrive(dy)
        if i + 1 < len(order):
            arrive(order[i + 1])
        to_sib[dy].wait_recv()
        block(around(y, -dy, ny))

    most = maxl[...] + bias[...].reshape(1, 1, voc)
    pool[p] = jnp.log1p(jax.nn.softplus(most)).reshape(rows, voc).astype(bf16)
    far_first = sorted(pass_peers, key=lambda d: -min(d[0], ny - d[0]))
    to_pool = {d: remote(pool.at[p], pool.at[p], pass_dev(*d)) for d in far_first}

    for copy in local[2:]:
        copy.wait()
    row, lane = iota((rows, 128), 0), iota((rows, 128), 1)
    in_group = lax.bitwise_and(row, PAD - 1)
    query = lax.shift_right_logical(row, 3) * group + in_group
    listed = jnp.broadcast_to(positive[...], (rows, positive.shape[1])).astype(f32)
    picked = jnp.where((query == lane) & (in_group < group), listed, 0.0)
    pos_col = jnp.sum(picked, axis=1, keepdims=True).astype(jnp.int32)
    is_pos = (lane + p * 128) == pos_col
    onehot = is_pos.astype(f32).astype(bf16)
    for j in range(n_pass):
        pos_s[j] = dot(onehot, pas[j]).astype(bf16)
    to_pos = {}
    for dy, dc in far_first:
        there = around(y, dy, ny) * NC + around(c, dc, NC)
        to_pos[dy, dc] = remote(pos_s.at[there], pos_r.at[dy * NC + dc], pass_dev(dy, dc))

    score = dot_nt(pool[p], pas[p])
    for dy, dc in reversed(far_first):
        to_pool[dy, dc].wait_recv()
        there = around(y, -dy, ny) * NC + around(c, -dc, NC)
        score = score + dot_nt(pool[there], pas[there])
    sc_s[...] = score.reshape(NX, PAD, 128)

    to_x = [remote(sc_s.at[around(x, d, NX)], sc_x.at[d], x_dev(d)) for d in range(1, NX)]
    for yy in range(ny):
        at = pl.multiple_of(yy * 256 + sib * 128, 128)
        ws_t[:, yy * 128:(yy + 1) * 128] = w_v[pl.ds(at, 128), :].T
        at = pl.multiple_of(yy * 256 + c * 128, 128)
        wo_t[:, yy * 128:(yy + 1) * 128] = w_v[pl.ds(at, 128), :].T
    mine = sc_s[x]
    for copy in to_x:
        copy.wait_recv()
    for d in range(1, NX):
        mine = mine + sc_x[d]
    zs[...] = mine
    to_z = [remote(zs, zr.at[d], z_dev(d)) for d in sorted(range(1, nz), key=lambda d: -min(d, nz - d))]
    gath_t[...] = gath[...].reshape(tok, gath.shape[2]).T
    prow = iota((tok, 128), 0)
    chunk = jnp.floor((prow.astype(f32) + 0.5) * (1.0 / ro)).astype(jnp.int32)
    zl = lax.bitwise_and(chunk, hz - 1)
    xx = lax.bitwise_and(lax.shift_right_logical(chunk, hz.bit_length() - 1), NX - 1)
    hh = lax.shift_right_logical(chunk, (hz * NX).bit_length() - 1)
    natural = prow + ro * ((hh * hz + zl) * NX + xx - chunk)
    plane = iota((tok, 128), 1)
    for j in range(tok // 128):
        perm[:, j * 128:(j + 1) * 128] = (natural == plane + j * 128).astype(f32).astype(bf16)
    at_sel = sell[...] + bias[...].reshape(1, 1, voc)
    slope[...] = (jax.nn.sigmoid(at_sel) / (1.0 + jax.nn.softplus(at_sel))).reshape(rows, voc)
    for copy in to_z:
        copy.wait_recv()
    for d in range(1, nz):
        mine = mine + zr[d]
    fin[x] = mine
    to_fin = [remote(fin.at[x], fin.at[x], x_dev(d)) for d in range(1, NX)]
    for copy in to_pos.values():
        copy.wait_recv()
    pos_entries = pos_s[p].astype(f32)
    for dy, dc in pass_peers:
        pos_entries = pos_entries + pos_r[dy * NC + dc].astype(f32)
    for copy in to_fin:
        copy.wait_recv()

    score = fin[...].reshape(rows, 128)
    peak = jnp.max(score, axis=1, keepdims=True)
    terms = jnp.exp(score - peak)
    other = jnp.where(is_pos, 0.0, terms)
    stats = [peak, jnp.sum(other, axis=1, keepdims=True),
             jnp.sum(jnp.where(is_pos, terms, 0.0), axis=1, keepdims=True),
             jnp.sum(jnp.where(is_pos, score, 0.0), axis=1, keepdims=True)]
    eye = row == lane
    turned = [jnp.sum(jnp.where(eye, s, 0.0), axis=0, keepdims=True) for s in stats]
    st_s[...] = jnp.concatenate(turned + [jnp.zeros((8 - len(turned), 128), f32)], axis=0)
    to_st = {d: remote(st_s, st.at[d[0] * NC + d[1]], pass_dev(*d)) for d in far_first}
    other = other.astype(bf16)
    to_u = {}
    for dy, dc in far_first:
        there = around(y, dy, ny) * NC + around(c, dc, NC)
        u_s[there] = dot(other, pas[there]).astype(bf16)
        to_u[dy, dc] = remote(u_s.at[there], u_r.at[dy * NC + dc], pass_dev(dy, dc))
    st[0] = st_s[...]
    mine_u = dot(other, pas[p])
    for copy in to_st.values():
        copy.wait_recv()
    peaks = [st[i][0:1] for i in range(n_pass)]
    top = functools.reduce(jnp.maximum, peaks)
    scale = [jnp.exp(k - top) for k in peaks]
    rest = sum(scale[i] * st[i][1:2] for i in range(n_pass))
    total = rest + sum(scale[i] * st[i][2:3] for i in range(n_pass))
    pos_score = sum(st[i][3:4] for i in range(n_pass))
    log_total = top + jnp.log(total)
    lane1 = iota((1, 128), 1)
    counted = (lax.bitwise_and(lane1, PAD - 1) < group) & (lane1 < rows)
    loss_o[...] = jnp.sum(jnp.where(counted, log_total - pos_score, 0.0), axis=1, keepdims=True) * (1.0 / n_queries)
    factor = (loss_scale / n_queries) / total

    def column(line):
        return jnp.sum(jnp.where(eye, line, 0.0), axis=1, keepdims=True)

    term = column(scale[0] * factor) * mine_u - column(rest * factor) * pos_entries
    for dy, dc in reversed(far_first):
        i = dy * NC + dc
        to_u[dy, dc].wait_recv()
        term = term + column(scale[i] * factor) * u_r[i].astype(f32)

    grad = term * slope[...]
    real = lax.bitwise_and(iota((rows, voc), 0), PAD - 1) < group
    gb_o[...] = jnp.sum(jnp.where(real, grad, 0.0), axis=0, keepdims=True)
    grad = grad.reshape(NX, PAD, voc)
    qlen = tok // n_queries
    at = iota((group, qlen, voc), 1)
    for g in range(NX):
        chosen = at == selp[g][0:group].reshape(group, 1, voc)
        some = jnp.where(chosen, grad[g][0:group].reshape(group, 1, voc), 0.0)
        lh[g * group * qlen:(g + 1) * group * qlen, :] = some.reshape(group * qlen, voc).astype(bf16)

    for h in range(2):
        lhp[h] = dot(perm[h * half:(h + 1) * half, :], lh[...]).astype(bf16)
    to_core = []
    for h in range(2):
        cs_s[h] = dot(lhp[h], ws_t[...]).astype(bf16)
        to_core.append(remote(cs_s.at[h], cs_r.at[h], pass_dev(0, 1)))
    for h in range(2):
        own[h] = dot(lhp[h], wo_t[...])
    to_core[0].wait_recv()
    both = own[0] + cs_r[0].astype(f32)
    for yy in range(ny):
        s1y[yy] = both[:, yy * 128:(yy + 1) * 128].astype(bf16)
    to_s1y = [remote(s1y.at[around(y, d, ny)], s1y_r.at[d], pass_dev(d, 0))
              for d in sorted(range(1, ny), key=lambda d: -min(d, ny - d))]
    to_core[1].wait_recv()
    both = own[1] + cs_r[1].astype(f32)
    for xx in range(NX):
        s1x[xx] = both[xx * part:(xx + 1) * part].astype(bf16)
    to_s1x = [remote(s1x.at[around(x, d, NX)], s1x_r.at[d], x_dev(d))
              for d in sorted(range(1, NX), key=lambda d: -min(d, NX - d))]

    gw_v[...] = dot(gath_t[...], lh[...])
    gw_out = pltpu.make_async_copy(gw_v, gw_o, loc_sems.at[0])
    gw_out.start()

    for copy in to_s1y:
        copy.wait_recv()
    both = s1y[y].astype(f32)
    for d in range(1, ny):
        both = both + s1y_r[d].astype(f32)
    s2x[...] = both.astype(bf16).reshape(NX, part, 128)
    to_s2x = [remote(s2x.at[around(x, d, NX)], s2x_r.at[d], x_dev(d)) for d in range(1, NX)]
    for copy in to_s1x:
        copy.wait_recv()
    both = s1x[x].astype(f32)
    for d in range(1, NX):
        both = both + s1x_r[d].astype(f32)
    for yy in range(ny):
        s2y[yy] = both[:, yy * 128:(yy + 1) * 128].astype(bf16)
    to_s2y = [remote(s2y.at[around(y, d, ny)], s2y_r.at[d], pass_dev(d, 0)) for d in range(1, ny)]
    for copy in to_s2x:
        copy.wait_recv()
    low = s2x[x].astype(f32)
    for d in range(1, NX):
        low = low + s2x_r[d].astype(f32)
    for k in range(hz):
        zf[k, 0:ro, :] = low[k * ro:(k + 1) * ro]
    for copy in to_s2y:
        copy.wait_recv()
    high = s2y[y].astype(f32)
    for d in range(1, ny):
        high = high + s2y_r[d].astype(f32)
    for k in range(hz):
        zf[hz + k, 0:ro, :] = high[k * ro:(k + 1) * ro]
    z2[...] = zf[...].astype(bf16)
    to_z2 = [remote(z2.at[around(z, d, nz)], z2_r.at[d], z_dev(d))
             for d in sorted(range(1, nz), key=lambda d: -min(d, nz - d))]
    total = zf[z]
    for copy in to_z2:
        copy.wait_recv()
    for d in range(1, nz):
        total = total + z2_r[d].astype(f32)
    gh_o[...] = total[0:ro].astype(bf16)

    for copy in started:
        copy.wait_send()
    gw_out.wait()


def local(nz, ny, hidden, weight, bias, token_ids, passages, positive, selected):
    n_queries, qlen = token_ids.shape
    own_rows, d = hidden.shape
    voc = weight.shape[1]
    n_pass = ny * NC
    tok = n_queries * qlen
    rows = NX * PAD
    hz = nz // 2
    ro = tok // (nz * NX)
    rp = -(-ro // 16) * 16
    part = hz * ro
    cols = ny * 128
    half = tok // 2
    n_copies = (2 * ny - 1) + 4 * (n_pass - 1) + 2 * (NX - 1) + 2 * (nz - 1) + 2 + 2 * (NX - 1) + 2 * (ny - 1)
    vmem = pl.BlockSpec(memory_space=pltpu.VMEM)
    anywhere = pl.BlockSpec(memory_space=pl.ANY)
    scratch = [
        ((n_pass, own_rows, d), bf16), ((d, tok), bf16), ((d, voc), bf16),
        ((voc, cols), bf16), ((voc, cols), bf16), ((n_pass, 128, voc), bf16), ((tok, tok), bf16),
        ((NX, PAD, voc), f32), ((NX, PAD, voc), f32), ((NX, PAD, voc), jnp.int32), ((NX, PAD, voc), jnp.int32),
        ((n_pass, rows, voc), bf16), ((n_pass, rows, voc), bf16), ((n_pass, rows, voc), bf16),
        ((NX, PAD, 128), f32), ((NX, PAD, 128), f32), ((PAD, 128), f32), ((nz, PAD, 128), f32),
        ((NX, PAD, 128), f32), ((8, 128), f32), ((n_pass, 8, 128), f32),
        ((n_pass, rows, voc), bf16), ((n_pass, rows, voc), bf16), ((rows, voc), f32),
        ((tok, voc), bf16), ((2, half, voc), bf16), ((2, half, cols), bf16), ((2, half, cols), bf16),
        ((2, half, cols), f32), ((ny, half, 128), bf16), ((ny, half, 128), bf16),
        ((NX, part, cols), bf16), ((NX, part, cols), bf16), ((NX, part, 128), bf16), ((NX, part, 128), bf16),
        ((ny, part, 128), bf16), ((ny, part, 128), bf16),
        ((nz, rp, 128), f32), ((nz, rp, 128), bf16), ((nz, rp, 128), bf16), ((d, voc), f32),
    ]
    loss, grad_hidden, grad_weight, grad_bias = pl.pallas_call(
        functools.partial(kernel, nz, ny, n_queries),
        out_shape=(
            jax.ShapeDtypeStruct((1, 1), f32),
            jax.ShapeDtypeStruct((ro, 128), bf16),
            jax.ShapeDtypeStruct((d, voc), f32),
            jax.ShapeDtypeStruct((1, voc), f32),
        ),
        in_specs=[anywhere, anywhere, vmem, vmem, anywhere, vmem, vmem],
        out_specs=(vmem, vmem, anywhere, vmem),
        scratch_shapes=[pltpu.VMEM(s, t) for s, t in scratch] + [
            pltpu.SemaphoreType.DMA((n_copies,)),
            pltpu.SemaphoreType.DMA((n_copies,)),
            pltpu.SemaphoreType.DMA((2 + n_pass,)),
        ],
        compiler_params=pltpu.CompilerParams(
            collective_id=0, has_side_effects=True, vmem_limit_bytes=48 * 1024 * 1024
        ),
    )(hidden, weight, bias.reshape(1, voc), token_ids, passages,
      jnp.pad(positive, (0, 128 - n_queries)).reshape(1, 128), selected)
    return loss.reshape(()), grad_hidden, grad_weight, grad_bias.reshape(voc)


def solution(mesh):
    in_specs = (
        P("pass", None),
        P(None, ("vocab", "pass")),
        P(("vocab", "pass")),
        P(),
        P("pass", "vocab"),
        P(),
        P(None, ("vocab", "pass")),
    )
    out_specs = (P(), P("vocab", "pass"), P(None, ("vocab", "pass")), P(("vocab", "pass")))
    body = functools.partial(local, mesh.shape["vocab"] // NX, mesh.shape["pass"] // NC)
    return jax.shard_map(body, mesh=mesh, in_specs=in_specs, out_specs=out_specs, check_vma=False)
```

time: 683 us -> 88.8 us (0.13)
  blocking collectives: 460 us -> 0 us
  waiting for transfers between devices: 131 us -> 0 us
  Pallas kernels: 0 us -> 77.7 us
  starting transfers between devices: 52.5 us -> 0 us
  between operations: 16.5 us -> 2.39 us
  matrix products: 9.41 us -> 0 us
    psum x2 -> x0, blocking collectives: 238 us -> none  [the longest x1 225 us: local(): scores = lax.psum(partial_value, 'vocab')]
    unnamed x1 -> x0, blocking collectives: 142 us -> none
    reduce_scatter x2 -> x0, waiting for transfers between devices: 90.8 us -> none  [the longest x1 61.2 us: local(): lax.psum_scatter(vocab_summed, 'pass', scatter_dimension=1, tiled=True)]
    pallas_call x0 -> x1, Pallas kernels: none -> 77.7 us  [local(): pl.pallas_call(functools.partial(kernel, nz, ny, n_queries), out_shape=(j...]
    pmax x1 -> x0, blocking collectives: 66.7 us -> none  [local(): peak_score = lax.pmax(jnp.max(scores, axis=1), 'pass')]
    unnamed x16 -> x0, starting transfers between devices: 52.4 us -> none
    all_gather x1 -> x0, waiting for transfers between devices: 39.2 us -> none  [local(): gathered = lax.all_gather(hidden, 'pass', axis=0, tiled=True)]
    all_gather x1 -> x0, blocking collectives: 12.9 us -> none  [local(): group_terms = lax.all_gather(pooled, 'pass', axis=1, tiled=True)]
  transfers between devices with their start and end apart: 19 -> 0, of which waited for: 3 -> 0; matrix products, arithmetic and copies ran while one was open for 1% -> 0% of each run, Pallas kernels for 0% -> 0%
where the time goes in v1:
time: 88.8 us; the launch traced here: 88.4 us
  Pallas kernels  77.7 us (88%)
  local copies, waits for them, and re-layouts  7.74 us (9%)
  between operations  2.39 us (3%)
    pallas_call x1, Pallas kernels, local(): pl.pallas_call(functools.partial(kernel, nz, ny, n_queries), out_shape=(j...  77.7 us
    unnamed x12, local copies, waits for them, and re-layouts  6.4 us

profile of v1, /device:TPU:1, one launch (start us, length us, event | category | flops | bytes accessed | tf_op | source)
XLA Modules:
  0.0 88.4 jit_solution(17970486889619421632)
XLA Ops:
  0.6 0.7 reshape.20.bias
  1.3 0.7 pad_bitcast_fusion.positive
  2.0 0.0 copy-start
  2.0 1.1 %copy-done = bf16[1024,384]{1,0:T(8,128)(2,1)S(1)} copy-done((bf16[1024,384]{1,0:T(8,128)(2,1)S(1)}, bf16[1024,384]{1,0:T(8,128)(2,1)}, u32[]{:S(2)}) %copy-start) | copy-done | bytes 786456
  3.1 0.0 copy-start.1
  3.1 1.1 %copy-done.1 = bf16[128,3072]{1,0:T(8,128)(2,1)S(1)} copy-done((bf16[128,3072]{1,0:T(8,128)(2,1)S(1)}, bf16[128,3072]{1,0:T(8,128)(2,1)}, u32[]{:S(2)}) %copy-start.1) | copy-done | bytes 786456
  4.2 0.0 copy-start.2
  4.2 0.9 %copy-done.2 = bf16[96,1024]{1,0:T(8,128)(2,1)S(1)} copy-done((bf16[96,1024]{1,0:T(8,128)(2,1)S(1)}, bf16[96,1024]{1,0:T(8,128)(2,1)}, u32[]{:S(2)}) %copy-start.2) | copy-done | bytes 196632
  5.2 0.0 copy-start.3
  5.2 0.8 copy-done.3
  5.9 0.0 copy-start.4
  5.9 0.7 copy-done.4
  6.6 77.7 %shard_map.102 = (f32[1,1]{1,0:T(1,128)}, bf16[12,128]{1,0:T(8,128)(2,1)S(1)}, f32[1024,384]{1,0:T(8,128)S(1)}, f32[1,384]{1,0:T(1,128)S(1)}) custom-call(bf16[96,1024]{1,0:T(8,128)(2,1)S(1)} %copy-done.2, bf16[1024,384]{1,0:T(8,128)(2,1)S(1)} %copy-done, f32[1,384]{1,0:T(1,128)S(1)} %reshape.20.bias, s32[24,32]{1,0:T(8,128)S(1)} %copy-done.4, ...), custom_call_target="tpu_custom_call" | custom-call | tf_op jit(solution)/shard_map/pallas_call | solution.py:359
  84.3 0.6 reduce
  85.5 0.6 copy.15
  86.1 1.1 %copy.16 = f32[1024,384]{1,0:T(8,128)} copy(f32[1024,384]{1,0:T(8,128)S(1)} %get-tuple-element.18) | data formatting | bytes 3145728
Async XLA Ops:
  2.0 1.1 %copy-start = (bf16[1024,384]{1,0:T(8,128)(2,1)S(1)}, bf16[1024,384]{1,0:T(8,128)(2,1)}, u32[]{:S(2)}) copy-start(bf16[1024,384]{1,0:T(8,128)(2,1)} %weight.1) | copy-start | bytes 2359300
  3.1 1.1 %copy-start.1 = (bf16[128,3072]{1,0:T(8,128)(2,1)S(1)}, bf16[128,3072]{1,0:T(8,128)(2,1)}, u32[]{:S(2)}) copy-start(bf16[128,3072]{1,0:T(8,128)(2,1)} %passages.1) | copy-start | bytes 2359300
  4.2 0.9 %copy-start.2 = (bf16[96,1024]{1,0:T(8,128)(2,1)S(1)}, bf16[96,1024]{1,0:T(8,128)(2,1)}, u32[]{:S(2)}) copy-start(bf16[96,1024]{1,0:T(8,128)(2,1)} %hidden.1) | copy-start | bytes 589828
  5.2 0.8 copy-start.3
  5.9 0.7 copy-start.4

commit v2 on v1

--- a/solution.py
+++ b/solution.py
@@ -33,7 +33,7 @@
            gath, gath_t, w_v, ws_t, wo_t, pas, perm, maxl, sell, selp, lenp,
            pool, pos_s, pos_r, sc_s, sc_x, zs, zr, fin, st_s, st, u_s, u_r, slope,
            lh, lhp, cs_s, cs_r, own, s1y, s1y_r, s1x, s1x_r, s2x, s2x_r, s2y, s2y_r,
-           zf, z2, z2_r, gw_v, send_sems, recv_sems, loc_sems):
+           zf, z2, z2_r, gw_v, bias_v, tokens_v, selected_v, send_sems, recv_sems, loc_sems):
     n_pass = ny * NC
     v = lax.axis_index("vocab")
     p = lax.axis_index("pass")
@@ -76,10 +76,13 @@
         return copy
 
     local = [pltpu.make_async_copy(hidden, gath.at[p], loc_sems.at[0]),
-             pltpu.make_async_copy(weight, w_v, loc_sems.at[1])]
+             pltpu.make_async_copy(weight, w_v, loc_sems.at[1]),
+             pltpu.make_async_copy(tokens, tokens_v, loc_sems.at[2]),
+             pltpu.make_async_copy(selected, selected_v, loc_sems.at[3]),
+             pltpu.make_async_copy(bias, bias_v, loc_sems.at[4])]
     for j in range(n_pass):
         local.append(pltpu.make_async_copy(
-            passages.at[:, pl.ds(j * voc, voc)], pas.at[j], loc_sems.at[2 + j]))
+            passages.at[:, pl.ds(j * voc, voc)], pas.at[j], loc_sems.at[5 + j]))
     for copy in local:
         copy.start()
 
@@ -100,10 +103,12 @@
     selp[...] = jnp.zeros_like(selp)
     lenp[...] = jnp.zeros_like(lenp)
     zf[...] = jnp.zeros_like(zf)
-    lengths = jnp.sum((tokens[...] != 1).astype(f32), axis=1, keepdims=True)
+    for copy in local[2:5]:
+        copy.wait()
+    lengths = jnp.sum((tokens_v[...] != 1).astype(f32), axis=1, keepdims=True)
     lengths = jnp.broadcast_to(lengths, (n_queries, voc))
     for g in range(NX):
-        selp[g, 0:group, :] = selected[g * group:(g + 1) * group, :]
+        selp[g, 0:group, :] = selected_v[g * group:(g + 1) * group, :]
         lenp[g, 0:group, :] = lengths[g * group:(g + 1) * group, :].astype(jnp.int32)
 
     def block(yy):
@@ -136,19 +141,20 @@
         to_sib[dy].wait_recv()
         block(around(y, -dy, ny))
 
-    most = maxl[...] + bias[...].reshape(1, 1, voc)
+    most = maxl[...] + bias_v[...].reshape(1, 1, voc)
     pool[p] = jnp.log1p(jax.nn.softplus(most)).reshape(rows, voc).astype(bf16)
     far_first = sorted(pass_peers, key=lambda d: -min(d[0], ny - d[0]))
     to_pool = {d: remote(pool.at[p], pool.at[p], pass_dev(*d)) for d in far_first}
 
-    for copy in local[2:]:
+    for copy in local[5:]:
         copy.wait()
     row, lane = iota((rows, 128), 0), iota((rows, 128), 1)
     in_group = lax.bitwise_and(row, PAD - 1)
     query = lax.shift_right_logical(row, 3) * group + in_group
-    listed = jnp.broadcast_to(positive[...], (rows, positive.shape[1])).astype(f32)
-    picked = jnp.where((query == lane) & (in_group < group), listed, 0.0)
-    pos_col = jnp.sum(picked, axis=1, keepdims=True).astype(jnp.int32)
+    query = jnp.where(in_group < group, query, -1)
+    pos_col = jnp.zeros((rows, 128), jnp.int32)
+    for q in range(n_queries):
+        pos_col = jnp.where(query == q, positive[q], pos_col)
     is_pos = (lane + p * 128) == pos_col
     onehot = is_pos.astype(f32).astype(bf16)
     for j in range(n_pass):
@@ -188,7 +194,7 @@
     plane = iota((tok, 128), 1)
     for j in range(tok // 128):
         perm[:, j * 128:(j + 1) * 128] = (natural == plane + j * 128).astype(f32).astype(bf16)
-    at_sel = sell[...] + bias[...].reshape(1, 1, voc)
+    at_sel = sell[...] + bias_v[...].reshape(1, 1, voc)
     slope[...] = (jax.nn.sigmoid(at_sel) / (1.0 + jax.nn.softplus(at_sel))).reshape(rows, voc)
     for copy in to_z:
         copy.wait_recv()
@@ -248,7 +254,7 @@
 
     grad = term * slope[...]
     real = lax.bitwise_and(iota((rows, voc), 0), PAD - 1) < group
-    gb_o[...] = jnp.sum(jnp.where(real, grad, 0.0), axis=0, keepdims=True)
+    gb_o[...] = jnp.sum(jnp.where(real, grad, 0.0), axis=0)
     grad = grad.reshape(NX, PAD, voc)
     qlen = tok // n_queries
     at = iota((group, qlen, voc), 1)
@@ -326,6 +332,15 @@
     gw_out.wait()
 
 
+def hand_out(*refs):
+    sems = refs[8]
+    copies = [pltpu.make_async_copy(refs[i], refs[4 + i], sems.at[i]) for i in range(4)]
+    for copy in copies:
+        copy.start()
+    for copy in copies:
+        copy.wait()
+
+
 def local(nz, ny, hidden, weight, bias, token_ids, passages, positive, selected):
     n_queries, qlen = token_ids.shape
     own_rows, d = hidden.shape
@@ -342,6 +357,7 @@
     n_copies = (2 * ny - 1) + 4 * (n_pass - 1) + 2 * (NX - 1) + 2 * (nz - 1) + 2 + 2 * (NX - 1) + 2 * (ny - 1)
     vmem = pl.BlockSpec(memory_space=pltpu.VMEM)
     anywhere = pl.BlockSpec(memory_space=pl.ANY)
+    hbm = pl.BlockSpec(memory_space=pltpu.HBM)
     scratch = [
         ((n_pass, own_rows, d), bf16), ((d, tok), bf16), ((d, voc), bf16),
         ((voc, cols), bf16), ((voc, cols), bf16), ((n_pass, 128, voc), bf16), ((tok, tok), bf16),
@@ -355,28 +371,36 @@
         ((NX, part, cols), bf16), ((NX, part, cols), bf16), ((NX, part, 128), bf16), ((NX, part, 128), bf16),
         ((ny, part, 128), bf16), ((ny, part, 128), bf16),
         ((nz, rp, 128), f32), ((nz, rp, 128), bf16), ((nz, rp, 128), bf16), ((d, voc), f32),
+        ((voc,), f32), ((n_queries, qlen), jnp.int32), ((n_queries, voc), jnp.int32),
     ]
-    loss, grad_hidden, grad_weight, grad_bias = pl.pallas_call(
+    results = pl.pallas_call(
         functools.partial(kernel, nz, ny, n_queries),
         out_shape=(
             jax.ShapeDtypeStruct((1, 1), f32),
             jax.ShapeDtypeStruct((ro, 128), bf16),
             jax.ShapeDtypeStruct((d, voc), f32),
-            jax.ShapeDtypeStruct((1, voc), f32),
+            jax.ShapeDtypeStruct((voc,), f32),
         ),
-        in_specs=[anywhere, anywhere, vmem, vmem, anywhere, vmem, vmem],
+        in_specs=[hbm, hbm, hbm, hbm, hbm, pl.BlockSpec(memory_space=pltpu.SMEM), hbm],
         out_specs=(vmem, vmem, anywhere, vmem),
         scratch_shapes=[pltpu.VMEM(s, t) for s, t in scratch] + [
             pltpu.SemaphoreType.DMA((n_copies,)),
             pltpu.SemaphoreType.DMA((n_copies,)),
-            pltpu.SemaphoreType.DMA((2 + n_pass,)),
+            pltpu.SemaphoreType.DMA((5 + n_pass,)),
         ],
         compiler_params=pltpu.CompilerParams(
             collective_id=0, has_side_effects=True, vmem_limit_bytes=48 * 1024 * 1024
         ),
-    )(hidden, weight, bias.reshape(1, voc), token_ids, passages,
-      jnp.pad(positive, (0, 128 - n_queries)).reshape(1, 128), selected)
-    return loss.reshape(()), grad_hidden, grad_weight, grad_bias.reshape(voc)
+    )(*(pltpu.with_memory_space_constraint(a, pltpu.HBM)
+        for a in (hidden, weight, bias, token_ids, passages, positive, selected)))
+    loss, grad_hidden, grad_weight, grad_bias = pl.pallas_call(
+        hand_out,
+        out_shape=tuple(jax.ShapeDtypeStruct(r.shape, r.dtype) for r in results),
+        in_specs=[anywhere] * 4,
+        out_specs=(hbm,) * 4,
+        scratch_shapes=[pltpu.SemaphoreType.DMA((4,))],
+    )(*results)
+    return loss.reshape(()), grad_hidden, grad_weight, grad_bias
 
 
 def solution(mesh):

time: 88.8 us -> 132 us (1.49)
  Pallas kernels: 77.7 us -> 129 us
  local copies, waits for them, and re-layouts: 7.74 us -> 2.34 us
  between operations: 2.39 us -> 0.65 us
    pallas_call x0 -> x1, Pallas kernels: none -> 49.6 us  [local(): pl.pallas_call(hand_out, out_shape=tuple((jax.ShapeDtypeStruct(r.shape, r...]
    unnamed x12 -> x6, local copies, waits for them, and re-layouts: 6.4 us -> 2.34 us
    pallas_call x1, Pallas kernels: 77.7 us -> 79.1 us  [local(): pl.pallas_call(functools.partial(kernel, nz, ny, n_queries), out_shape=(j...]
    reshape x2 -> x0, local copies, waits for them, and re-layouts: 1.34 us -> none  [the longest x1 0.68 us: local(): bias.reshape(1, voc)]
where the time goes in v2:
time: 132 us
  Pallas kernels  129 us (98%)
  local copies, waits for them, and re-layouts  2.34 us (2%)
    pallas_call x1, Pallas kernels, local(): pl.pallas_call(functools.partial(kernel, nz, ny, n_queries), out_shape=(j...  79.1 us
    pallas_call x1, Pallas kernels, local(): pl.pallas_call(hand_out, out_shape=tuple((jax.ShapeDtypeStruct(r.shape, r...  49.6 us

profile of v2, /device:TPU:1, one launch (start us, length us, event | category | flops | bytes accessed | tf_op | source)
XLA Modules:
  0.0 131.6 jit_solution(8314323812913364642)
XLA Ops:
  0.6 79.1 %shard_map.102 = (f32[1,1]{1,0:T(1,128)}, bf16[12,128]{1,0:T(8,128)(2,1)S(1)}, f32[1024,384]{1,0:T(8,128)S(1)}, f32[384]{0:T(512)S(1)}) custom-call(bf16[96,1024]{1,0:T(8,128)(2,1)} %hidden.1, bf16[1024,384]{1,0:T(8,128)(2,1)} %weight.1, f32[384]{0:T(512)} %bias.1, s32[24,32]{1,0:T(8,128)} %tokens.1, bf16[128,3072]{1,0:T(8,128)(2,1)} %passages.1, ...), custom_call_target="tpu_custom_call" | custom-call | tf_op jit(solution)/shard_map/pallas_call | solution.py:376
  79.7 0.0 copy-start
  79.7 1.2 copy-done
  80.9 0.0 copy-start.1
  80.9 0.6 copy-done.1
  81.5 0.0 copy-start.2
  81.5 0.6 copy-done.2
  82.1 49.6 %shard_map.103 = (f32[1,1]{1,0:T(1,128)}, bf16[12,128]{1,0:T(8,128)(2,1)}, f32[1024,384]{1,0:T(8,128)}, f32[384]{0:T(512)}) custom-call(f32[1,1]{1,0:T(1,128)} %get-tuple-element.12.refs_0_, bf16[12,128]{1,0:T(8,128)(2,1)} %copy-done.1, f32[1024,384]{1,0:T(8,128)} %copy-done, f32[384]{0:T(512)} %copy-done.2), custom_call_target="tpu_custom_call" | custom-call | tf_op jit(solution)/shard_map/pallas_call | solution.py:396
Async XLA Ops:
  79.7 1.2 copy-start
  80.9 0.6 copy-start.1
  81.5 0.6 copy-start.2

commit v3 on v0

v3 whole, which is shorter than its diff:
```python
import functools

import jax
import jax.numpy as jnp
from jax import lax
from jax.experimental import pallas as pl
from jax.experimental.pallas import tpu as pltpu
from jax.sharding import PartitionSpec as P

loss_scale = 4096.0
NX = 4
NC = 2
SLOT = 4
ROWS = 16
MAX_COPIES = 112
MESH = pl.DeviceIdType.MESH
f32 = jnp.float32
bf16 = jnp.bfloat16


def dot(a, b):
    return jnp.dot(a, b, preferred_element_type=f32)


def iota(shape, axis):
    return lax.broadcasted_iota(jnp.int32, shape, axis)


def near_last(size):
    return sorted(range(1, size), key=lambda d: -min(d, size - d))


def kernel(nz, ny, n_queries, hidden, weight, bias, tokens, passages, positive, selected,
           loss_o, gh_o, gw_o, gb_o,
           gath, gath_o, gath_t, w_v, w_t, pas, pas_t, perm, bias_v, bias_b, tokens_v, sel_v, selp, lenp,
           maxl, sell, maxa, sela, pool, pos_s, pos_r, sc_s, sc_x, zs, zr, fin, st_s, st, u_s, u_r, slope,
           lh, lh_o, lhp, gs, gs_r, s1y, s1y_r, s1x, s1x_r, s2x, s2x_r, s2y, s2y_r, high,
           zf, z2, z2_r, gw_v, send_sems, recv_sems, loc_sems):
    n_pass = ny * NC
    v = lax.axis_index("vocab")
    p = lax.axis_index("pass")
    z, x = lax.div(v, NX), lax.rem(v, NX)
    y, c = lax.div(p, NC), lax.rem(p, NC)
    sib = 1 - c
    own_rows = gath.shape[1]
    d_model = gath.shape[2]
    voc = w_v.shape[1] // NC
    wide = NC * voc
    qlen = tokens_v.shape[1]
    per_block = n_queries // n_pass
    tok = ny * own_rows
    half = tok // 2
    ro = (NC * tok) // (nz * NX)
    per_half = nz // 4
    z_block = nz // n_pass
    part = per_half * ro
    tile = sc_s.shape[1]

    def around(value, shift, size):
        return lax.rem(value + (shift + size), size)

    def pass_index(dy, dc):
        return around(y, dy, ny) * NC + around(c, dc, NC)

    def pass_dev(dy, dc):
        return (v, pass_index(dy, dc))

    def x_dev(dx):
        return (z * NX + around(x, dx, NX), p)

    def z_dev(dz):
        return (around(z, dz, nz) * NX + x, p)

    sibling = (v, y * NC + sib)
    pass_peers = [(dy, dc) for dy in near_last(ny) + [0] for dc in range(NC) if dy or dc]
    y_far, x_far, z_far = near_last(ny), near_last(NX), near_last(nz)
    started = []

    def remote(src, dst, device):
        i = len(started)
        copy = pltpu.make_async_remote_copy(
            src_ref=src, dst_ref=dst, send_sem=send_sems.at[i], recv_sem=recv_sems.at[i],
            device_id=device, device_id_type=MESH,
        )
        copy.start()
        started.append(copy)
        return copy

    mine = pl.ds(pl.multiple_of(c * voc, 128), voc)
    theirs = pl.ds(pl.multiple_of(sib * voc, 128), voc)
    mine_pas = pl.ds(pl.multiple_of(c * 128, 128), 128)
    local = [pltpu.make_async_copy(bias, bias_v, loc_sems.at[0]),
             pltpu.make_async_copy(tokens, tokens_v, loc_sems.at[1]),
             pltpu.make_async_copy(selected, sel_v.at[c], loc_sems.at[2]),
             pltpu.make_async_copy(hidden, gath.at[y], loc_sems.at[3]),
             pltpu.make_async_copy(weight, w_v.at[:, mine], loc_sems.at[4])]
    for j in range(ny):
        local.append(pltpu.make_async_copy(
            passages.at[:, pl.ds(j * wide, wide)], pas.at[j, mine_pas], loc_sems.at[5 + j]))
    for copy in local:
        copy.start()

    barrier = pltpu.get_barrier_semaphore()
    peers = ([z_dev(d) for d in z_far] + [x_dev(d) for d in x_far] + [pass_dev(*d) for d in pass_peers])
    for device in peers:
        pl.semaphore_signal(barrier, inc=1, device_id=device, device_id_type=MESH)
    for ref in (maxl, sell, maxa, sela, selp, lenp, zf):
        ref[...] = jnp.zeros_like(ref)
    for copy in local[:3]:
        copy.wait()
    bias_b[c] = jnp.broadcast_to(bias_v[...].reshape(1, voc), (8, voc))
    pl.semaphore_wait(barrier, len(peers))

    hr = own_rows // 2
    top, bottom = pl.ds(0, hr), pl.ds(hr, hr)
    if ny == 4:
        first_up = remote(hidden.at[top], gath.at[y, top], pass_dev(1, 0))
        first_down = remote(hidden.at[bottom], gath.at[y, bottom], pass_dev(-1, 0))
        then_up = remote(hidden.at[bottom], gath.at[y, bottom], pass_dev(1, 0))
        then_down = remote(hidden.at[top], gath.at[y, top], pass_dev(-1, 0))
    else:
        direct = [remote(hidden, gath.at[y], pass_dev(d, 0)) for d in y_far]
    to_w = remote(weight, w_v.at[:, mine], sibling)
    to_small = [remote(selected, sel_v.at[c], sibling), remote(bias_b.at[c], bias_b.at[c], sibling)]
    to_pas = [remote(passages.at[:, pl.ds(j * wide, wide)], pas.at[j, mine_pas], sibling) for j in range(ny)]

    lengths = jnp.sum((tokens_v[...] != 1).astype(f32), axis=1, keepdims=True).astype(jnp.int32)
    lengths = jnp.broadcast_to(lengths, (n_queries, wide))
    for copy in to_small:
        copy.wait_recv()
    picks = jnp.concatenate([sel_v[0], sel_v[1]], axis=1)
    for j in range(ny):
        a = 2 * j * per_block
        b = a + per_block
        selp[j, 0:per_block, :] = jnp.where(c == 0, picks[a:b], picks[b:b + per_block])
        lenp[j, 0:per_block, :] = jnp.where(c == 0, lengths[a:b], lengths[b:b + per_block])

    def block(yy):
        logits = dot(gath[yy], w_v[...]).reshape(per_block, qlen, wide)
        at = iota((per_block, qlen, wide), 1)
        valid = at < lenp[yy][0:per_block].reshape(per_block, 1, wide)
        chosen = at == selp[yy][0:per_block].reshape(per_block, 1, wide)
        maxl[yy, 0:per_block, :] = jnp.max(jnp.where(valid, logits, -jnp.inf), axis=1)
        sell[yy, 0:per_block, :] = jnp.sum(jnp.where(chosen, logits, 0.0), axis=1)

    local[3].wait()
    local[4].wait()
    if ny == 4:
        up, down, far = around(y, -1, ny), around(y, 1, ny), around(y, 2, ny)
        first_up.wait_recv()
        relay_up = remote(gath.at[up, top], gath.at[up, top], pass_dev(1, 0))
        first_down.wait_recv()
        relay_down = remote(gath.at[down, bottom], gath.at[down, bottom], pass_dev(-1, 0))
        to_w.wait_recv()
        block(y)
        then_up.wait_recv()
        block(up)
        then_down.wait_recv()
        block(down)
    else:
        to_w.wait_recv()
        block(y)
    for copy in local[5:]:
        copy.wait()
    for copy in to_pas:
        copy.wait_recv()
    for j in range(ny):
        pas_t[j] = pas[j].T
    if ny == 4:
        relay_up.wait_recv()
        relay_down.wait_recv()
        block(far)
    else:
        for d, copy in zip(y_far, direct):
            copy.wait_recv()
            block(around(y, -d, ny))

    wide_bias = jnp.concatenate([bias_b[0], bias_b[1]], axis=1)[0:1]
    for j in range(ny):
        maxa[j * SLOT:(j + 1) * SLOT, :] = maxl[j, 0:SLOT, :]
    pool[y] = jnp.log1p(jax.nn.softplus(maxa[...] + wide_bias)).astype(bf16)
    to_pool = {d: remote(pool.at[y], pool.at[y], pass_dev(d, 0)) for d in y_far}
    row, lane = iota((ROWS, 256), 0), iota((ROWS, 256), 1)
    place = lax.bitwise_and(row, SLOT - 1)
    query = (lax.shift_right_logical(row, 2) * NC + c) * per_block + place
    query = jnp.where((place < per_block) & (row < ny * SLOT), query, -1)
    pos_col = jnp.zeros((ROWS, 256), jnp.int32)
    for q in range(n_queries):
        pos_col = jnp.where(query == q, positive[q], pos_col)
    is_pos = (lane + y * 256) == pos_col
    onehot = is_pos.astype(f32).astype(bf16)

    score = dot(pool[y], pas_t[y])
    for d in reversed(y_far):
        to_pool[d].wait_recv()
        there = around(y, -d, ny)
        score = score + dot(pool[there], pas_t[there])

    for j in range(NX):
        a, b = (j // 2) * tile, (j % 2) * 128
        sc_s[j] = score[a:a + tile, b:b + 128]
    to_x = [remote(sc_s.at[around(x, d, NX)], sc_x.at[d], x_dev(d)) for d in x_far]
    for j in range(ny):
        pos_s[j] = dot(onehot, pas[j]).astype(bf16)
    to_pos = [remote(pos_s.at[around(y, d, ny)], pos_r.at[d], pass_dev(d, 0)) for d in y_far]
    to_other = remote(gath, gath_o, sibling)
    total = sc_s[x]
    for copy in to_x:
        copy.wait_recv()
    for d in range(1, NX):
        total = total + sc_x[d]
    zs[...] = total
    to_z = [remote(zs, zr.at[d], z_dev(d)) for d in z_far]
    w_t[...] = w_v[...].T
    prow = iota((tok, 128), 0)
    chunk = jnp.floor((prow.astype(f32) + 0.5) * (1.0 / ro)).astype(jnp.int32)
    zl = lax.bitwise_and(chunk, per_half - 1)
    xx = lax.bitwise_and(lax.shift_right_logical(chunk, per_half.bit_length() - 1), NX - 1)
    hh = lax.shift_right_logical(chunk, (per_half * NX).bit_length() - 1)
    natural = prow + ro * ((hh * per_half + zl) * NX + xx - chunk)
    plane = iota((tok, 128), 1)
    for j in range(tok // 128):
        perm[:, j * 128:(j + 1) * 128] = (natural == plane + j * 128).astype(f32).astype(bf16)
    for j in range(ny):
        sela[j * SLOT:(j + 1) * SLOT, :] = sell[j, 0:SLOT, :]
    at_sel = sela[...] + wide_bias
    slope[...] = jax.nn.sigmoid(at_sel) / (1.0 + jax.nn.softplus(at_sel))
    gath_t[0] = gath[...].reshape(tok, d_model).T
    for copy in to_z:
        copy.wait_recv()
    for d in range(1, nz):
        total = total + zr[d]
    fin[x] = total
    to_fin = [remote(fin.at[x], fin.at[x], x_dev(d)) for d in x_far]
    for copy in to_pos:
        copy.wait_recv()
    pos_entries = pos_s[y].astype(f32)
    for d in range(1, ny):
        pos_entries = pos_entries + pos_r[d].astype(f32)
    for copy in to_fin:
        copy.wait_recv()

    score = jnp.concatenate([jnp.concatenate([fin[j], fin[j + 1]], axis=1) for j in range(0, NX, 2)], axis=0)
    peak = jnp.max(score, axis=1, keepdims=True)
    terms = jnp.exp(score - peak)
    other = jnp.where(is_pos, 0.0, terms)
    stats = [peak, jnp.sum(other, axis=1, keepdims=True),
             jnp.sum(jnp.where(is_pos, terms, 0.0), axis=1, keepdims=True),
             jnp.sum(jnp.where(is_pos, score, 0.0), axis=1, keepdims=True)]
    eye = iota((ROWS, 128), 0) == iota((ROWS, 128), 1)
    turned = [jnp.sum(jnp.where(eye, s, 0.0), axis=0, keepdims=True) for s in stats]
    st_s[...] = jnp.concatenate(turned + [jnp.zeros((8 - len(turned), 128), f32)], axis=0)
    other = other.astype(bf16)
    to_u = {}
    for d in y_far:
        there = around(y, d, ny)
        u_s[there] = dot(other, pas[there]).astype(bf16)
        to_u[d] = remote(u_s.at[there], u_r.at[d], pass_dev(d, 0))
    to_st = [remote(st_s, st.at[d], pass_dev(d, 0)) for d in y_far]
    st[0] = st_s[...]
    mine_u = dot(other, pas[y])
    for copy in to_st:
        copy.wait_recv()
    peaks = [st[i][0:1] for i in range(ny)]
    highest = functools.reduce(jnp.maximum, peaks)
    scale = [jnp.exp(k - highest) for k in peaks]
    rest = sum(scale[i] * st[i][1:2] for i in range(ny))
    denom = rest + sum(scale[i] * st[i][2:3] for i in range(ny))
    pos_score = sum(st[i][3:4] for i in range(ny))
    log_total = highest + jnp.log(denom)
    lane1 = iota((1, 128), 1)
    counted = (lax.bitwise_and(lane1, SLOT - 1) < per_block) & (lane1 < ny * SLOT)
    loss = jnp.sum(jnp.where(counted, log_total - pos_score, 0.0), axis=1, keepdims=True)
    factor = (loss_scale / n_queries) / denom

    def column(line):
        return jnp.sum(jnp.where(eye, line, 0.0), axis=1, keepdims=True)

    term = column(scale[0] * factor) * mine_u - column(rest * factor) * pos_entries
    for d in reversed(y_far):
        to_u[d].wait_recv()
        term = term + column(scale[d] * factor) * u_r[d].astype(f32)

    grad = term * slope[...]
    at = iota((per_block, qlen, wide), 1)
    for j in range(ny):
        chosen = at == selp[j][0:per_block].reshape(per_block, 1, wide)
        some = grad[j * SLOT:j * SLOT + per_block].reshape(per_block, 1, wide)
        lh[j * own_rows:(j + 1) * own_rows, :] = jnp.where(chosen, some, 0.0).reshape(own_rows, wide).astype(bf16)

    lhp[0] = dot(perm[0:half, :], lh[...]).astype(bf16)
    out = dot(lhp[0], w_t[...])
    for j in range(n_pass):
        s1y[j] = out[:, j * 128:(j + 1) * 128].astype(bf16)
    to_s1y = {d: remote(s1y.at[pass_index(*d)], s1y_r.at[d[0] * NC + d[1]], pass_dev(*d)) for d in pass_peers}
    lhp[1] = dot(perm[half:tok, :], lh[...]).astype(bf16)
    out = dot(lhp[1], w_t[...])
    for j in range(NX):
        s1x[j] = out[j * part:(j + 1) * part].astype(bf16)
    to_s1x = [remote(s1x.at[around(x, d, NX)], s1x_r.at[d], x_dev(d)) for d in x_far]

    at_row = iota((ROWS, wide), 0)
    real = (lax.bitwise_and(at_row, SLOT - 1) < per_block) & (at_row < ny * SLOT)
    summed = jnp.sum(jnp.where(real, grad, 0.0), axis=0, keepdims=True)
    first = iota((8, voc), 0) == 0
    for j in range(NC):
        gs[j] = jnp.where(first, summed[:, j * voc:(j + 1) * voc], loss)
    to_gs = remote(gs.at[sib], gs_r, sibling)
    to_lh = remote(lh.at[:, theirs], lh_o, sibling)
    to_other.wait_recv()
    gath_t[1] = gath_o[...].reshape(tok, d_model).T
    gw_v[...] = dot(gath_t[0], lh[:, mine])

    for copy in to_s1y.values():
        copy.wait_recv()
    same, cross = s1y[p].astype(f32), s1y_r[1].astype(f32)
    for d in range(1, ny):
        same = same + s1y_r[d * NC].astype(f32)
        cross = cross + s1y_r[d * NC + 1].astype(f32)
    s2x[c] = same.astype(bf16).reshape(NX, part, 128)
    s2x[sib] = cross.astype(bf16).reshape(NX, part, 128)
    to_s2x = [remote(s2x.at[:, around(x, d, NX)], s2x_r.at[d], x_dev(d)) for d in x_far]
    for copy in to_s1x:
        copy.wait_recv()
    both = s1x[x].astype(f32)
    for d in range(1, NX):
        both = both + s1x_r[d].astype(f32)
    for j in range(n_pass):
        s2y[j] = both[:, j * 128:(j + 1) * 128].astype(bf16)
    to_s2y = {d: remote(s2y.at[pass_index(*d)], s2y_r.at[d[0] * NC + d[1]], pass_dev(*d)) for d in pass_peers}
    for copy in to_s2x:
        copy.wait_recv()

    def to_rows(core, k):
        return (NC * (k // z_block) + core) * z_block + k % z_block

    for core in range(NC):
        low = s2x[core, x].astype(f32)
        for d in range(1, NX):
            low = low + s2x_r[d, core].astype(f32)
        for k in range(per_half):
            zf[to_rows(core, k), 0:ro, :] = low[k * ro:(k + 1) * ro]
    for copy in to_s2y.values():
        copy.wait_recv()
    same, cross = s2y[p].astype(f32), s2y_r[1].astype(f32)
    for d in range(1, ny):
        same = same + s2y_r[d * NC].astype(f32)
        cross = cross + s2y_r[d * NC + 1].astype(f32)
    high[c] = same
    high[sib] = cross
    for core in range(NC):
        for k in range(per_half):
            zf[to_rows(core, per_half + k), 0:ro, :] = high[core, k * ro:(k + 1) * ro]
    z2[...] = zf[...].astype(bf16)
    to_z2 = [remote(z2.at[around(z, d, nz)], z2_r.at[d], z_dev(d)) for d in z_far]
    to_lh.wait_recv()
    gw_v[...] += dot(gath_t[1], lh_o[...])
    gw_out = pltpu.make_async_copy(gw_v, gw_o, loc_sems.at[0])
    gw_out.start()
    to_gs.wait_recv()
    gb_o[...] = (gs[c][0:1] + gs_r[0:1]).reshape(voc)
    loss_o[...] = (gs[c][1:2, 0:1] + gs_r[1:2, 0:1]) * (1.0 / n_queries)
    total = zf[z]
    for copy in to_z2:
        copy.wait_recv()
    for d in range(1, nz):
        total = total + z2_r[d].astype(f32)
    gh_o[...] = total[0:ro].astype(bf16)

    for copy in started:
        copy.wait_send()
    gw_out.wait()


def hand_out(*refs):
    sems = refs[8]
    copies = [pltpu.make_async_copy(refs[i], refs[4 + i], sems.at[i]) for i in range(4)]
    for copy in copies:
        copy.start()
    for copy in copies:
        copy.wait()


def local(nz, ny, hidden, weight, bias, token_ids, passages, positive, selected):
    n_queries, qlen = token_ids.shape
    own_rows, d = hidden.shape
    voc = weight.shape[1]
    wide = NC * voc
    n_pass = ny * NC
    tok = ny * own_rows
    half = tok // 2
    ro = (NC * tok) // (nz * NX)
    rp = -(-ro // 16) * 16
    part = (nz // 4) * ro
    tile = ROWS * 2 // NX
    i32 = jnp.int32
    vmem = pl.BlockSpec(memory_space=pltpu.VMEM)
    smem = pl.BlockSpec(memory_space=pltpu.SMEM)
    anywhere = pl.BlockSpec(memory_space=pl.ANY)
    hbm = pl.BlockSpec(memory_space=pltpu.HBM)
    scratch = [
        ((ny, own_rows, d), bf16), ((ny, own_rows, d), bf16), ((NC, d, tok), bf16),
        ((d, wide), bf16), ((wide, d), bf16),
        ((ny, NC * 128, wide), bf16), ((ny, wide, NC * 128), bf16), ((tok, tok), bf16),
        ((voc,), f32), ((NC, 8, voc), f32), ((n_queries, qlen), i32), ((NC, n_queries, voc), i32),
        ((ny, 8, wide), i32), ((ny, 8, wide), i32),
        ((ny, 8, wide), f32), ((ny, 8, wide), f32), ((ROWS, wide), f32), ((ROWS, wide), f32),
        ((ny, ROWS, wide), bf16), ((ny, ROWS, wide), bf16), ((ny, ROWS, wide), bf16),
        ((NX, tile, 128), f32), ((NX, tile, 128), f32), ((tile, 128), f32), ((nz, tile, 128), f32),
        ((NX, tile, 128), f32), ((8, 128), f32), ((ny, 8, 128), f32),
        ((ny, ROWS, wide), bf16), ((ny, ROWS, wide), bf16), ((ROWS, wide), f32),
        ((tok, wide), bf16), ((tok, voc), bf16), ((2, half, wide), bf16),
        ((NC, 8, voc), f32), ((8, voc), f32),
        ((n_pass, half, 128), bf16), ((n_pass, half, 128), bf16),
        ((NX, part, d), bf16), ((NX, part, d), bf16),
        ((NC, NX, part, 128), bf16), ((NX, NC, part, 128), bf16),
        ((n_pass, part, 128), bf16), ((n_pass, part, 128), bf16), ((NC, part, 128), f32),
        ((nz, rp, 128), f32), ((nz, rp, 128), bf16), ((nz, rp, 128), bf16), ((d, voc), f32),
    ]
    results = pl.pallas_call(
        functools.partial(kernel, nz, ny, n_queries),
        out_shape=(
            jax.ShapeDtypeStruct((1, 1), f32),
            jax.ShapeDtypeStruct((ro, 128), bf16),
            jax.ShapeDtypeStruct((d, voc), f32),
            jax.ShapeDtypeStruct((voc,), f32),
        ),
        in_specs=[hbm, hbm, hbm, hbm, hbm, smem, hbm],
        out_specs=(vmem, vmem, anywhere, vmem),
        scratch_shapes=[pltpu.VMEM(s, t) for s, t in scratch] + [
            pltpu.SemaphoreType.DMA((MAX_COPIES,)),
            pltpu.SemaphoreType.DMA((MAX_COPIES,)),
            pltpu.SemaphoreType.DMA((5 + ny,)),
        ],
        compiler_params=pltpu.CompilerParams(
            collective_id=0, has_side_effects=True, vmem_limit_bytes=48 * 1024 * 1024
        ),
    )(*(pltpu.with_memory_space_constraint(a, pltpu.HBM)
        for a in (hidden, weight, bias, token_ids, passages, positive, selected)))
    loss, grad_hidden, grad_weight, grad_bias = pl.pallas_call(
        hand_out,
        out_shape=tuple(jax.ShapeDtypeStruct(r.shape, r.dtype) for r in results),
        in_specs=[vmem] * 4,
        out_specs=(hbm,) * 4,
        scratch_shapes=[pltpu.SemaphoreType.DMA((4,))],
    )(*results)
    return loss.reshape(()), grad_hidden, grad_weight, grad_bias


def solution(mesh):
    in_specs = (
        P("pass", None),
        P(None, ("vocab", "pass")),
        P(("vocab", "pass")),
        P(),
        P("pass", "vocab"),
        P(),
        P(None, ("vocab", "pass")),
    )
    out_specs = (P(), P("vocab", "pass"), P(None, ("vocab", "pass")), P(("vocab", "pass")))
    body = functools.partial(local, mesh.shape["vocab"] // NX, mesh.shape["pass"] // NC)
    return jax.shard_map(body, mesh=mesh, in_specs=in_specs, out_specs=out_specs, check_vma=False)
```

time: 683 us -> 77.3 us (0.11)
  blocking collectives: 460 us -> 0 us
  waiting for transfers between devices: 131 us -> 0 us
  Pallas kernels: 0 us -> 74.1 us
  starting transfers between devices: 52.5 us -> 0 us
  between operations: 16.5 us -> 0.65 us
  matrix products: 9.41 us -> 0 us
    psum x2 -> x0, blocking collectives: 238 us -> none  [the longest x1 225 us: local(): scores = lax.psum(partial_value, 'vocab')]
    unnamed x1 -> x0, blocking collectives: 142 us -> none
    reduce_scatter x2 -> x0, waiting for transfers between devices: 90.8 us -> none  [the longest x1 61.2 us: local(): lax.psum_scatter(vocab_summed, 'pass', scatter_dimension=1, tiled=True)]
    pallas_call x0 -> x2, Pallas kernels: none -> 74.1 us  [the longest x1 70.9 us: local(): pl.pallas_call(functools.partial(kernel, nz, ny, n_queries), out_shape=(j...]
    pmax x1 -> x0, blocking collectives: 66.7 us -> none  [local(): peak_score = lax.pmax(jnp.max(scores, axis=1), 'pass')]
    unnamed x16 -> x0, starting transfers between devices: 52.4 us -> none
    all_gather x1 -> x0, waiting for transfers between devices: 39.2 us -> none  [local(): gathered = lax.all_gather(hidden, 'pass', axis=0, tiled=True)]
    all_gather x1 -> x0, blocking collectives: 12.9 us -> none  [local(): group_terms = lax.all_gather(pooled, 'pass', axis=1, tiled=True)]
  transfers between devices with their start and end apart: 19 -> 0, of which waited for: 3 -> 0; matrix products, arithmetic and copies ran while one was open for 1% -> 0% of each run, Pallas kernels for 0% -> 0%
where the time goes in v3:
time: 77.3 us; the launch traced here: 77.1 us
  Pallas kernels  74.1 us (96%)
  local copies, waits for them, and re-layouts  2.34 us (3%)
    pallas_call x1, Pallas kernels, local(): pl.pallas_call(functools.partial(kernel, nz, ny, n_queries), out_shape=(j...  70.9 us
    pallas_call x1, Pallas kernels, local(): pl.pallas_call(hand_out, out_shape=tuple((jax.ShapeDtypeStruct(r.shape, r...  3.22 us
    unnamed x6, local copies, waits for them, and re-layouts  2.34 us

profile of v3, /device:TPU:1, one launch (start us, length us, event | category | flops | bytes accessed | tf_op | source)
XLA Modules:
  0.0 77.1 jit_solution(18162425320166915760)
XLA Ops:
  0.6 70.9 %shard_map.102 = (f32[1,1]{1,0:T(1,128)}, bf16[12,128]{1,0:T(8,128)(2,1)S(1)}, f32[1024,384]{1,0:T(8,128)S(1)}, f32[384]{0:T(512)S(1)}) custom-call(bf16[96,1024]{1,0:T(8,128)(2,1)} %hidden.1, bf16[1024,384]{1,0:T(8,128)(2,1)} %weight.1, f32[384]{0:T(512)} %bias.1, s32[24,32]{1,0:T(8,128)} %tokens.1, bf16[128,3072]{1,0:T(8,128)(2,1)} %passages.1, ...), custom_call_target="tpu_custom_call" | custom-call | tf_op jit(solution)/shard_map/pallas_call | solution.py:420
  71.5 0.0 copy-start
  71.5 1.2 %copy-done = f32[1024,384]{1,0:T(8,128)} copy-done((f32[1024,384]{1,0:T(8,128)}, f32[1024,384]{1,0:T(8,128)S(1)}, u32[]{:S(2)}) %copy-start) | copy-done | bytes 1572888
  72.7 0.0 copy-start.1
  72.7 0.6 copy-done.1
  73.3 0.0 copy-start.2
  73.3 0.6 copy-done.2
  73.9 3.2 %shard_map.103 = (f32[1,1]{1,0:T(1,128)}, bf16[12,128]{1,0:T(8,128)(2,1)}, f32[1024,384]{1,0:T(8,128)}, f32[384]{0:T(512)}) custom-call(f32[1,1]{1,0:T(1,128)} %get-tuple-element.12.refs_0_, bf16[12,128]{1,0:T(8,128)(2,1)} %copy-done.1, f32[1024,384]{1,0:T(8,128)} %copy-done, f32[384]{0:T(512)} %copy-done.2), custom_call_target="tpu_custom_call" | custom-call | tf_op jit(solution)/shard_map/pallas_call | solution.py:440
Async XLA Ops:
  71.5 1.2 %copy-start = (f32[1024,384]{1,0:T(8,128)}, f32[1024,384]{1,0:T(8,128)S(1)}, u32[]{:S(2)}) copy-start(f32[1024,384]{1,0:T(8,128)S(1)} %get-tuple-element.14.refs_2_) | copy-start | bytes 4718596
  72.7 0.6 copy-start.1
  73.3 0.6 copy-start.2

commit v4 on v3

--- a/solution.py
+++ b/solution.py
@@ -35,7 +35,7 @@
            gath, gath_o, gath_t, w_v, w_t, pas, pas_t, perm, bias_v, bias_b, tokens_v, sel_v, selp, lenp,
            maxl, sell, maxa, sela, pool, pos_s, pos_r, sc_s, sc_x, zs, zr, fin, st_s, st, u_s, u_r, slope,
            lh, lh_o, lhp, gs, gs_r, s1y, s1y_r, s1x, s1x_r, s2x, s2x_r, s2y, s2y_r, high,
-           zf, z2, z2_r, gw_v, send_sems, recv_sems, loc_sems):
+           zf, z2, z2_r, gw_v, send_sems, recv_sems, loc_sems, entry):
     n_pass = ny * NC
     v = lax.axis_index("vocab")
     p = lax.axis_index("pass")
@@ -101,28 +101,50 @@
         copy.start()
 
     barrier = pltpu.get_barrier_semaphore()
-    peers = ([z_dev(d) for d in z_far] + [x_dev(d) for d in x_far] + [pass_dev(*d) for d in pass_peers])
+    passed_on = nz == 16
+    z_near = (2, -2, 1, -1) if passed_on else z_far
+    peers = ([z_dev(d) for d in z_near] + [pass_dev(*d) for d in pass_peers] + [x_dev(d) for d in x_far])
     for device in peers:
         pl.semaphore_signal(barrier, inc=1, device_id=device, device_id_type=MESH)
-    for ref in (maxl, sell, maxa, sela, selp, lenp, zf):
-        ref[...] = jnp.zeros_like(ref)
-    for copy in local[:3]:
-        copy.wait()
-    bias_b[c] = jnp.broadcast_to(bias_v[...].reshape(1, voc), (8, voc))
     pl.semaphore_wait(barrier, len(peers))
 
     hr = own_rows // 2
     top, bottom = pl.ds(0, hr), pl.ds(hr, hr)
     if ny == 4:
-        first_up = remote(hidden.at[top], gath.at[y, top], pass_dev(1, 0))
-        first_down = remote(hidden.at[bottom], gath.at[y, bottom], pass_dev(-1, 0))
+        pieces = [(pl.ds(i, 16), pl.ds(hr + i, 16)) for i in range(0, hr, 16)]
+        first = []
+        for a, b in pieces:
+            first.append((remote(hidden.at[a], gath.at[y, a], pass_dev(1, 0)),
+                          remote(hidden.at[b], gath.at[y, b], pass_dev(-1, 0))))
         then_up = remote(hidden.at[bottom], gath.at[y, bottom], pass_dev(1, 0))
         then_down = remote(hidden.at[top], gath.at[y, top], pass_dev(-1, 0))
     else:
         direct = [remote(hidden, gath.at[y], pass_dev(d, 0)) for d in y_far]
+    if passed_on:
+        pl.semaphore_signal(entry.at[0], inc=1, device_id=z_dev(2), device_id_type=MESH)
+        pl.semaphore_signal(entry.at[1], inc=1, device_id=z_dev(-2), device_id_type=MESH)
     to_w = remote(weight, w_v.at[:, mine], sibling)
+    for copy in local[:3]:
+        copy.wait()
+    bias_b[c] = jnp.broadcast_to(bias_v[...].reshape(1, voc), (8, voc))
     to_small = [remote(selected, sel_v.at[c], sibling), remote(bias_b.at[c], bias_b.at[c], sibling)]
     to_pas = [remote(passages.at[:, pl.ds(j * wide, wide)], pas.at[j, mine_pas], sibling) for j in range(ny)]
+
+    if ny == 4:
+        up, down, far = around(y, -1, ny), around(y, 1, ny), around(y, 2, ny)
+        relayed = []
+        for (a, b), (to_up, to_down) in zip(pieces, first):
+            to_up.wait_recv()
+            relayed.append(remote(gath.at[up, a], gath.at[up, a], pass_dev(1, 0)))
+            to_down.wait_recv()
+            relayed.append(remote(gath.at[down, b], gath.at[down, b], pass_dev(-1, 0)))
+    if passed_on:
+        pl.semaphore_wait(entry.at[0], 1)
+        pl.semaphore_wait(entry.at[1], 1)
+        pl.semaphore_signal(entry.at[2], inc=1, device_id=z_dev(4), device_id_type=MESH)
+        pl.semaphore_signal(entry.at[3], inc=1, device_id=z_dev(-4), device_id_type=MESH)
+    for ref in (maxl, sell, maxa, sela, selp, lenp, zf):
+        ref[...] = jnp.zeros_like(ref)
 
     lengths = jnp.sum((tokens_v[...] != 1).astype(f32), axis=1, keepdims=True).astype(jnp.int32)
     lengths = jnp.broadcast_to(lengths, (n_queries, wide))
@@ -146,11 +168,6 @@
     local[3].wait()
     local[4].wait()
     if ny == 4:
-        up, down, far = around(y, -1, ny), around(y, 1, ny), around(y, 2, ny)
-        first_up.wait_recv()
-        relay_up = remote(gath.at[up, top], gath.at[up, top], pass_dev(1, 0))
-        first_down.wait_recv()
-        relay_down = remote(gath.at[down, bottom], gath.at[down, bottom], pass_dev(-1, 0))
         to_w.wait_recv()
         block(y)
         then_up.wait_recv()
@@ -167,8 +184,8 @@
     for j in range(ny):
         pas_t[j] = pas[j].T
     if ny == 4:
-        relay_up.wait_recv()
-        relay_down.wait_recv()
+        for copy in relayed:
+            copy.wait_recv()
         block(far)
     else:
         for d, copy in zip(y_far, direct):
@@ -210,6 +227,9 @@
     for d in range(1, NX):
         total = total + sc_x[d]
     zs[...] = total
+    if passed_on:
+        pl.semaphore_wait(entry.at[2], 1)
+        pl.semaphore_wait(entry.at[3], 1)
     to_z = [remote(zs, zr.at[d], z_dev(d)) for d in z_far]
     w_t[...] = w_v[...].T
     prow = iota((tok, 128), 0)
@@ -353,6 +373,8 @@
             zf[to_rows(core, per_half + k), 0:ro, :] = high[core, k * ro:(k + 1) * ro]
     z2[...] = zf[...].astype(bf16)
     to_z2 = [remote(z2.at[around(z, d, nz)], z2_r.at[d], z_dev(d)) for d in z_far]
+    for copy in started[:-len(to_z2)]:
+        copy.wait_send()
     to_lh.wait_recv()
     gw_v[...] += dot(gath_t[1], lh_o[...])
     gw_out = pltpu.make_async_copy(gw_v, gw_o, loc_sems.at[0])
@@ -367,7 +389,7 @@
         total = total + z2_r[d].astype(f32)
     gh_o[...] = total[0:ro].astype(bf16)
 
-    for copy in started:
+    for copy in to_z2:
         copy.wait_send()
     gw_out.wait()
 
@@ -431,6 +453,7 @@
             pltpu.SemaphoreType.DMA((MAX_COPIES,)),
             pltpu.SemaphoreType.DMA((MAX_COPIES,)),
             pltpu.SemaphoreType.DMA((5 + ny,)),
+            pltpu.SemaphoreType.REGULAR((4,)),
         ],
         compiler_params=pltpu.CompilerParams(
             collective_id=0, has_side_effects=True, vmem_limit_bytes=48 * 1024 * 1024
@@ -440,9 +463,10 @@
     loss, grad_hidden, grad_weight, grad_bias = pl.pallas_call(
         hand_out,
         out_shape=tuple(jax.ShapeDtypeStruct(r.shape, r.dtype) for r in results),
-        in_specs=[vmem] * 4,
+        in_specs=[anywhere] * 4,
         out_specs=(hbm,) * 4,
         scratch_shapes=[pltpu.SemaphoreType.DMA((4,))],
+        compiler_params=pltpu.CompilerParams(vmem_limit_bytes=1024 * 1024),
     )(*results)
     return loss.reshape(()), grad_hidden, grad_weight, grad_bias
 

time: 77.3 us -> 68.8 us (0.89)
  Pallas kernels: 74.1 us -> 68 us
  local copies, waits for them, and re-layouts: 2.34 us -> 0 us
    pallas_call x1, Pallas kernels: 70.9 us -> 66.2 us  [local(): pl.pallas_call(functools.partial(kernel, nz, ny, n_queries), out_shape=(j...]
    unnamed x6 -> x0, local copies, waits for them, and re-layouts: 2.34 us -> none
    pallas_call x1, Pallas kernels: 3.22 us -> 1.82 us  [local(): pl.pallas_call(hand_out, out_shape=tuple((jax.ShapeDtypeStruct(r.shape, r...]
where the time goes in v4:
time: 68.8 us; the launch traced here: 68.6 us
  Pallas kernels  68 us (99%)
    pallas_call x1, Pallas kernels, local(): pl.pallas_call(functools.partial(kernel, nz, ny, n_queries), out_shape=(j...  66.2 us
    pallas_call x1, Pallas kernels, local(): pl.pallas_call(hand_out, out_shape=tuple((jax.ShapeDtypeStruct(r.shape, r...  1.82 us

profile of v4, /device:TPU:1, one launch (start us, length us, event | category | flops | bytes accessed | tf_op | source)
XLA Modules:
  0.0 68.6 jit_solution(3854527234013703402)
XLA Ops:
  0.6 66.2 %shard_map.102 = (f32[1,1]{1,0:T(1,128)}, bf16[12,128]{1,0:T(8,128)(2,1)S(1)}, f32[1024,384]{1,0:T(8,128)S(1)}, f32[384]{0:T(512)S(1)}) custom-call(bf16[96,1024]{1,0:T(8,128)(2,1)} %hidden.1, bf16[1024,384]{1,0:T(8,128)(2,1)} %weight.1, f32[384]{0:T(512)} %bias.1, s32[24,32]{1,0:T(8,128)} %tokens.1, bf16[128,3072]{1,0:T(8,128)(2,1)} %passages.1, ...), custom_call_target="tpu_custom_call" | custom-call | tf_op jit(solution)/shard_map/pallas_call | solution.py:442
  66.8 1.8 %shard_map.103 = (f32[1,1]{1,0:T(1,128)}, bf16[12,128]{1,0:T(8,128)(2,1)}, f32[1024,384]{1,0:T(8,128)}, f32[384]{0:T(512)}) custom-call(f32[1,1]{1,0:T(1,128)} %get-tuple-element.12.refs_0_, bf16[12,128]{1,0:T(8,128)(2,1)S(1)} %get-tuple-element.13.refs_1_, f32[1024,384]{1,0:T(8,128)S(1)} %get-tuple-element.14.refs_2_, f32[384]{0:T(512)S(1)} %get-tuple-element.15.refs_3_), custom_call_target="tpu_custom_call" | custom-call | tf_op jit(solution)/shard_map/pallas_call | solution.py:463

commit v5 on v4

--- a/solution.py
+++ b/solution.py
@@ -32,9 +32,9 @@
 
 def kernel(nz, ny, n_queries, hidden, weight, bias, tokens, passages, positive, selected,
            loss_o, gh_o, gw_o, gb_o,
-           gath, gath_o, gath_t, w_v, w_t, pas, pas_t, perm, bias_v, bias_b, tokens_v, sel_v, selp, lenp,
+           gath, gath_o, gath_t, w_v, wr, wr_t, pas, pas_t, perm, bias_v, bias_b, tokens_v, sel_v, selp, lenp,
            maxl, sell, maxa, sela, pool, pos_s, pos_r, sc_s, sc_x, zs, zr, fin, st_s, st, u_s, u_r, slope,
-           lh, lh_o, lhp, gs, gs_r, s1y, s1y_r, s1x, s1x_r, s2x, s2x_r, s2y, s2y_r, high,
+           sel_r, g_r, lh, lh_y, lh_o, gs, gs_r, s1, s1_r, high,
            zf, z2, z2_r, gw_v, send_sems, recv_sems, loc_sems, entry):
     n_pass = ny * NC
     v = lax.axis_index("vocab")
@@ -49,11 +49,11 @@
     qlen = tokens_v.shape[1]
     per_block = n_queries // n_pass
     tok = ny * own_rows
-    half = tok // 2
     ro = (NC * tok) // (nz * NX)
-    per_half = nz // 4
+    per_core = nz // 2
     z_block = nz // n_pass
-    part = per_half * ro
+    part = per_core * ro
+    chip_cols = NC * 128
     tile = sc_s.shape[1]
 
     def around(value, shift, size):
@@ -65,14 +65,14 @@
     def pass_dev(dy, dc):
         return (v, pass_index(dy, dc))
 
-    def x_dev(dx):
-        return (z * NX + around(x, dx, NX), p)
+    def x_dev(dx, dc=0):
+        return (z * NX + around(x, dx, NX), pass_index(0, dc))
 
     def z_dev(dz):
         return (around(z, dz, nz) * NX + x, p)
 
     sibling = (v, y * NC + sib)
-    pass_peers = [(dy, dc) for dy in near_last(ny) + [0] for dc in range(NC) if dy or dc]
+    x_peers = [(dx, dc) for dx in near_last(NX) + [0] for dc in range(NC) if dx or dc]
     y_far, x_far, z_far = near_last(ny), near_last(NX), near_last(nz)
     started = []
 
@@ -103,7 +103,7 @@
     barrier = pltpu.get_barrier_semaphore()
     passed_on = nz == 16
     z_near = (2, -2, 1, -1) if passed_on else z_far
-    peers = ([z_dev(d) for d in z_near] + [pass_dev(*d) for d in pass_peers] + [x_dev(d) for d in x_far])
+    peers = ([z_dev(d) for d in z_near] + [pass_dev(d, 0) for d in y_far] + [x_dev(*d) for d in x_peers])
     for device in peers:
         pl.semaphore_signal(barrier, inc=1, device_id=device, device_id_type=MESH)
     pl.semaphore_wait(barrier, len(peers))
@@ -220,6 +220,13 @@
     for j in range(ny):
         pos_s[j] = dot(onehot, pas[j]).astype(bf16)
     to_pos = [remote(pos_s.at[around(y, d, ny)], pos_r.at[d], pass_dev(d, 0)) for d in y_far]
+    to_wr = {}
+    for d in y_far:
+        rows = pl.ds(pl.multiple_of(around(y, d, ny) * chip_cols, chip_cols), chip_cols)
+        to_wr[d] = remote(w_v.at[rows, mine], wr.at[y, :, mine], pass_dev(d, 0))
+    for j in range(ny):
+        sel_r[y, j * SLOT:(j + 1) * SLOT, :] = selp[j, 0:SLOT, :]
+    to_sel = [remote(sel_r.at[y], sel_r.at[y], pass_dev(d, 0)) for d in y_far]
     to_other = remote(gath, gath_o, sibling)
     total = sc_s[x]
     for copy in to_x:
@@ -231,13 +238,12 @@
         pl.semaphore_wait(entry.at[2], 1)
         pl.semaphore_wait(entry.at[3], 1)
     to_z = [remote(zs, zr.at[d], z_dev(d)) for d in z_far]
-    w_t[...] = w_v[...].T
+    wr_t[y] = w_v[pl.ds(pl.multiple_of(y * chip_cols, chip_cols), chip_cols), :].T
     prow = iota((tok, 128), 0)
     chunk = jnp.floor((prow.astype(f32) + 0.5) * (1.0 / ro)).astype(jnp.int32)
-    zl = lax.bitwise_and(chunk, per_half - 1)
-    xx = lax.bitwise_and(lax.shift_right_logical(chunk, per_half.bit_length() - 1), NX - 1)
-    hh = lax.shift_right_logical(chunk, (per_half * NX).bit_length() - 1)
-    natural = prow + ro * ((hh * per_half + zl) * NX + xx - chunk)
+    zl = lax.bitwise_and(chunk, per_core - 1)
+    xx = lax.shift_right_logical(chunk, per_core.bit_length() - 1)
+    natural = prow + ro * (zl * NX + xx - chunk)
     plane = iota((tok, 128), 1)
     for j in range(tok // 128):
         perm[:, j * 128:(j + 1) * 128] = (natural == plane + j * 128).astype(f32).astype(bf16)
@@ -252,6 +258,11 @@
         total = total + zr[d]
     fin[x] = total
     to_fin = [remote(fin.at[x], fin.at[x], x_dev(d)) for d in x_far]
+    to_wr_sib = []
+    for d in reversed(y_far):
+        to_wr[d].wait_recv()
+        there = around(y, -d, ny)
+        to_wr_sib.append(remote(wr.at[there, :, mine], wr.at[there, :, mine], sibling))
     for copy in to_pos:
         copy.wait_recv()
     pos_entries = pos_s[y].astype(f32)
@@ -279,6 +290,10 @@
     to_st = [remote(st_s, st.at[d], pass_dev(d, 0)) for d in y_far]
     st[0] = st_s[...]
     mine_u = dot(other, pas[y])
+    for d, copy in zip(reversed(y_far), to_wr_sib):
+        copy.wait_recv()
+        there = around(y, -d, ny)
+        wr_t[there] = wr[there].T
     for copy in to_st:
         copy.wait_recv()
     peaks = [st[i][0:1] for i in range(ny)]
@@ -302,22 +317,34 @@
         term = term + column(scale[d] * factor) * u_r[d].astype(f32)
 
     grad = term * slope[...]
+    g_r[y] = grad.astype(bf16)
+    to_g = {d: remote(g_r.at[y], g_r.at[y], pass_dev(d, 0)) for d in y_far}
     at = iota((per_block, qlen, wide), 1)
-    for j in range(ny):
-        chosen = at == selp[j][0:per_block].reshape(per_block, 1, wide)
-        some = grad[j * SLOT:j * SLOT + per_block].reshape(per_block, 1, wide)
-        lh[j * own_rows:(j + 1) * own_rows, :] = jnp.where(chosen, some, 0.0).reshape(own_rows, wide).astype(bf16)
-
-    lhp[0] = dot(perm[0:half, :], lh[...]).astype(bf16)
-    out = dot(lhp[0], w_t[...])
-    for j in range(n_pass):
-        s1y[j] = out[:, j * 128:(j + 1) * 128].astype(bf16)
-    to_s1y = {d: remote(s1y.at[pass_index(*d)], s1y_r.at[d[0] * NC + d[1]], pass_dev(*d)) for d in pass_peers}
-    lhp[1] = dot(perm[half:tok, :], lh[...]).astype(bf16)
-    out = dot(lhp[1], w_t[...])
-    for j in range(NX):
-        s1x[j] = out[j * part:(j + 1) * part].astype(bf16)
-    to_s1x = [remote(s1x.at[around(x, d, NX)], s1x_r.at[d], x_dev(d)) for d in x_far]
+
+    def spread(yy, out):
+        taken, picks = g_r[yy].astype(f32), sel_r[yy]
+        for j in range(ny):
+            some = taken[j * SLOT:j * SLOT + per_block].reshape(per_block, 1, wide)
+            chosen = at == picks[j * SLOT:j * SLOT + per_block].reshape(per_block, 1, wide)
+            out[j * own_rows:(j + 1) * own_rows, :] = jnp.where(chosen, some, 0.0).reshape(own_rows, wide).astype(bf16)
+
+    spread(y, lh)
+    to_lh = remote(lh.at[:, theirs], lh_o, sibling)
+
+    out = dot(lh[...], wr_t[y])
+    for copy in to_sel:
+        copy.wait_recv()
+    for d in reversed(y_far):
+        to_g[d].wait_recv()
+        there = around(y, -d, ny)
+        spread(there, lh_y)
+        out = out + dot(lh_y[...], wr_t[there])
+    out = dot(perm[...], out.astype(bf16)).astype(bf16)
+    for k in range(NC):
+        for j in range(NX):
+            s1[k, j] = out[j * part:(j + 1) * part, k * 128:(k + 1) * 128]
+    to_s1 = [remote(s1.at[around(c, dc, NC), around(x, dx, NX)], s1_r.at[dx * NC + dc], x_dev(dx, dc))
+             for dx, dc in x_peers]
 
     at_row = iota((ROWS, wide), 0)
     real = (lax.bitwise_and(at_row, SLOT - 1) < per_block) & (at_row < ny * SLOT)
@@ -326,51 +353,22 @@
     for j in range(NC):
         gs[j] = jnp.where(first, summed[:, j * voc:(j + 1) * voc], loss)
     to_gs = remote(gs.at[sib], gs_r, sibling)
-    to_lh = remote(lh.at[:, theirs], lh_o, sibling)
     to_other.wait_recv()
     gath_t[1] = gath_o[...].reshape(tok, d_model).T
     gw_v[...] = dot(gath_t[0], lh[:, mine])
 
-    for copy in to_s1y.values():
-        copy.wait_recv()
-    same, cross = s1y[p].astype(f32), s1y_r[1].astype(f32)
-    for d in range(1, ny):
-        same = same + s1y_r[d * NC].astype(f32)
-        cross = cross + s1y_r[d * NC + 1].astype(f32)
-    s2x[c] = same.astype(bf16).reshape(NX, part, 128)
-    s2x[sib] = cross.astype(bf16).reshape(NX, part, 128)
-    to_s2x = [remote(s2x.at[:, around(x, d, NX)], s2x_r.at[d], x_dev(d)) for d in x_far]
-    for copy in to_s1x:
-        copy.wait_recv()
-    both = s1x[x].astype(f32)
+    for copy in to_s1:
+        copy.wait_recv()
+    same, cross = s1[c, x].astype(f32), s1_r[1].astype(f32)
     for d in range(1, NX):
-        both = both + s1x_r[d].astype(f32)
-    for j in range(n_pass):
-        s2y[j] = both[:, j * 128:(j + 1) * 128].astype(bf16)
-    to_s2y = {d: remote(s2y.at[pass_index(*d)], s2y_r.at[d[0] * NC + d[1]], pass_dev(*d)) for d in pass_peers}
-    for copy in to_s2x:
-        copy.wait_recv()
-
-    def to_rows(core, k):
-        return (NC * (k // z_block) + core) * z_block + k % z_block
-
-    for core in range(NC):
-        low = s2x[core, x].astype(f32)
-        for d in range(1, NX):
-            low = low + s2x_r[d, core].astype(f32)
-        for k in range(per_half):
-            zf[to_rows(core, k), 0:ro, :] = low[k * ro:(k + 1) * ro]
-    for copy in to_s2y.values():
-        copy.wait_recv()
-    same, cross = s2y[p].astype(f32), s2y_r[1].astype(f32)
-    for d in range(1, ny):
-        same = same + s2y_r[d * NC].astype(f32)
-        cross = cross + s2y_r[d * NC + 1].astype(f32)
+        same = same + s1_r[d * NC].astype(f32)
+        cross = cross + s1_r[d * NC + 1].astype(f32)
     high[c] = same
     high[sib] = cross
     for core in range(NC):
-        for k in range(per_half):
-            zf[to_rows(core, per_half + k), 0:ro, :] = high[core, k * ro:(k + 1) * ro]
+        for k in range(per_core):
+            to_row = (NC * (k // z_block) + core) * z_block + k % z_block
+            zf[to_row, 0:ro, :] = high[core, k * ro:(k + 1) * ro]
     z2[...] = zf[...].astype(bf16)
     to_z2 = [remote(z2.at[around(z, d, nz)], z2_r.at[d], z_dev(d)) for d in z_far]
     for copy in started[:-len(to_z2)]:
@@ -408,12 +406,10 @@
     own_rows, d = hidden.shape
     voc = weight.shape[1]
     wide = NC * voc
-    n_pass = ny * NC
     tok = ny * own_rows
-    half = tok // 2
     ro = (NC * tok) // (nz * NX)
     rp = -(-ro // 16) * 16
-    part = (nz // 4) * ro
+    part = (nz // 2) * ro
     tile = ROWS * 2 // NX
     i32 = jnp.int32
     vmem = pl.BlockSpec(memory_space=pltpu.VMEM)
@@ -422,7 +418,7 @@
     hbm = pl.BlockSpec(memory_space=pltpu.HBM)
     scratch = [
         ((ny, own_rows, d), bf16), ((ny, own_rows, d), bf16), ((NC, d, tok), bf16),
-        ((d, wide), bf16), ((wide, d), bf16),
+        ((d, wide), bf16), ((ny, NC * 128, wide), bf16), ((ny, wide, NC * 128), bf16),
         ((ny, NC * 128, wide), bf16), ((ny, wide, NC * 128), bf16), ((tok, tok), bf16),
         ((voc,), f32), ((NC, 8, voc), f32), ((n_queries, qlen), i32), ((NC, n_queries, voc), i32),
         ((ny, 8, wide), i32), ((ny, 8, wide), i32),
@@ -431,12 +427,10 @@
         ((NX, tile, 128), f32), ((NX, tile, 128), f32), ((tile, 128), f32), ((nz, tile, 128), f32),
         ((NX, tile, 128), f32), ((8, 128), f32), ((ny, 8, 128), f32),
         ((ny, ROWS, wide), bf16), ((ny, ROWS, wide), bf16), ((ROWS, wide), f32),
-        ((tok, wide), bf16), ((tok, voc), bf16), ((2, half, wide), bf16),
+        ((ny, ROWS, wide), i32), ((ny, ROWS, wide), bf16),
+        ((tok, wide), bf16), ((tok, wide), bf16), ((tok, voc), bf16),
         ((NC, 8, voc), f32), ((8, voc), f32),
-        ((n_pass, half, 128), bf16), ((n_pass, half, 128), bf16),
-        ((NX, part, d), bf16), ((NX, part, d), bf16),
-        ((NC, NX, part, 128), bf16), ((NX, NC, part, 128), bf16),
-        ((n_pass, part, 128), bf16), ((n_pass, part, 128), bf16), ((NC, part, 128), f32),
+        ((NC, NX, part, 128), bf16), ((NX * NC, part, 128), bf16), ((NC, part, 128), f32),
         ((nz, rp, 128), f32), ((nz, rp, 128), bf16), ((nz, rp, 128), bf16), ((d, voc), f32),
     ]
     results = pl.pallas_call(

time: 68.8 us -> 67 us (0.974)
  Pallas kernels: 68 us -> 66.2 us
    pallas_call x1, Pallas kernels: 66.2 us -> 64.4 us  [local(): pl.pallas_call(functools.partial(kernel, nz, ny, n_queries), out_shape=(j...]
where the time goes in v5:
time: 67 us; the launch traced here: 66.9 us
  Pallas kernels  66.2 us (99%)
    pallas_call x1, Pallas kernels, local(): pl.pallas_call(functools.partial(kernel, nz, ny, n_queries), out_shape=(j...  64.4 us
    pallas_call x1, Pallas kernels, local(): pl.pallas_call(hand_out, out_shape=tuple((jax.ShapeDtypeStruct(r.shape, r...  1.82 us

profile of v5, /device:TPU:1, one launch (start us, length us, event | category | flops | bytes accessed | tf_op | source)
XLA Modules:
  0.0 66.9 jit_solution(3218844598009588352)
XLA Ops:
  0.6 64.4 %shard_map.102 = (f32[1,1]{1,0:T(1,128)}, bf16[12,128]{1,0:T(8,128)(2,1)S(1)}, f32[1024,384]{1,0:T(8,128)S(1)}, f32[384]{0:T(512)S(1)}) custom-call(bf16[96,1024]{1,0:T(8,128)(2,1)} %hidden.1, bf16[1024,384]{1,0:T(8,128)(2,1)} %weight.1, f32[384]{0:T(512)} %bias.1, s32[24,32]{1,0:T(8,128)} %tokens.1, bf16[128,3072]{1,0:T(8,128)(2,1)} %passages.1, ...), custom_call_target="tpu_custom_call" | custom-call | tf_op jit(solution)/shard_map/pallas_call | solution.py:436
  65.0 1.8 %shard_map.103 = (f32[1,1]{1,0:T(1,128)}, bf16[12,128]{1,0:T(8,128)(2,1)}, f32[1024,384]{1,0:T(8,128)}, f32[384]{0:T(512)}) custom-call(f32[1,1]{1,0:T(1,128)} %get-tuple-element.12.refs_0_, bf16[12,128]{1,0:T(8,128)(2,1)S(1)} %get-tuple-element.13.refs_1_, f32[1024,384]{1,0:T(8,128)S(1)} %get-tuple-element.14.refs_2_, f32[384]{0:T(512)S(1)} %get-tuple-element.15.refs_3_), custom_call_target="tpu_custom_call" | custom-call | tf_op jit(solution)/shard_map/pallas_call | solution.py:457

commit v6 on v5

--- a/solution.py
+++ b/solution.py
@@ -12,7 +12,7 @@
 NC = 2
 SLOT = 4
 ROWS = 16
-MAX_COPIES = 112
+MAX_SEMS = 37
 MESH = pl.DeviceIdType.MESH
 f32 = jnp.float32
 bf16 = jnp.bfloat16
@@ -30,9 +30,9 @@
     return sorted(range(1, size), key=lambda d: -min(d, size - d))
 
 
-def kernel(nz, ny, n_queries, hidden, weight, bias, tokens, passages, positive, selected,
+def kernel(nz, ny, n_queries, hidden, weight, bias, tokens, passages, positive_h, selected,
            loss_o, gh_o, gw_o, gb_o,
-           gath, gath_o, gath_t, w_v, wr, wr_t, pas, pas_t, perm, bias_v, bias_b, tokens_v, sel_v, selp, lenp,
+           gath, gath_o, gath_t, w_v, wr, wr_t, pas, pas_t, perm, bias_v, bias_b, positive, tokens_v, sel_v, selp, lenp,
            maxl, sell, maxa, sela, pool, pos_s, pos_r, sc_s, sc_x, zs, zr, fin, st_s, st, u_s, u_r, slope,
            sel_r, g_r, lh, lh_y, lh_o, gs, gs_r, s1, s1_r, high,
            zf, z2, z2_r, gw_v, send_sems, recv_sems, loc_sems, entry):
@@ -74,17 +74,35 @@
     sibling = (v, y * NC + sib)
     x_peers = [(dx, dc) for dx in near_last(NX) + [0] for dc in range(NC) if dx or dc]
     y_far, x_far, z_far = near_last(ny), near_last(NX), near_last(nz)
-    started = []
-
-    def remote(src, dst, device):
-        i = len(started)
-        copy = pltpu.make_async_remote_copy(
+    started, taken_sems = [], []
+
+    def take():
+        taken_sems.append(0)
+        return len(taken_sems) - 1
+
+    def describe(src, dst, device, i):
+        return pltpu.make_async_remote_copy(
             src_ref=src, dst_ref=dst, send_sem=send_sems.at[i], recv_sem=recv_sems.at[i],
             device_id=device, device_id_type=MESH,
         )
+
+    def remote(src, dst, device, i=None):
+        copy = describe(src, dst, device, take() if i is None else i)
         copy.start()
-        started.append(copy)
+        if i is None:
+            started.append(copy)
         return copy
+
+    def together(i, ref):
+        whole = describe(ref, ref, sibling, i)
+        started.append(whole)
+        return whole
+
+    def remotes(copies, ref):
+        i = take()
+        for src, dst, device in copies:
+            remote(src, dst, device, i)
+        return together(i, ref)
 
     mine = pl.ds(pl.multiple_of(c * voc, 128), voc)
     theirs = pl.ds(pl.multiple_of(sib * voc, 128), voc)
@@ -97,6 +115,7 @@
     for j in range(ny):
         local.append(pltpu.make_async_copy(
             passages.at[:, pl.ds(j * wide, wide)], pas.at[j, mine_pas], loc_sems.at[5 + j]))
+    local.append(pltpu.make_async_copy(positive_h, positive, loc_sems.at[5 + ny]))
     for copy in local:
         copy.start()
 
@@ -128,16 +147,18 @@
         copy.wait()
     bias_b[c] = jnp.broadcast_to(bias_v[...].reshape(1, voc), (8, voc))
     to_small = [remote(selected, sel_v.at[c], sibling), remote(bias_b.at[c], bias_b.at[c], sibling)]
-    to_pas = [remote(passages.at[:, pl.ds(j * wide, wide)], pas.at[j, mine_pas], sibling) for j in range(ny)]
+    to_pas = remotes([(passages.at[:, pl.ds(j * wide, wide)], pas.at[j, mine_pas], sibling) for j in range(ny)],
+                     pas.at[pl.ds(0, ny // 2)])
 
     if ny == 4:
         up, down, far = around(y, -1, ny), around(y, 1, ny), around(y, 2, ny)
-        relayed = []
+        i = take()
         for (a, b), (to_up, to_down) in zip(pieces, first):
             to_up.wait_recv()
-            relayed.append(remote(gath.at[up, a], gath.at[up, a], pass_dev(1, 0)))
+            remote(gath.at[up, a], gath.at[up, a], pass_dev(1, 0), i)
             to_down.wait_recv()
-            relayed.append(remote(gath.at[down, b], gath.at[down, b], pass_dev(-1, 0)))
+            remote(gath.at[down, b], gath.at[down, b], pass_dev(-1, 0), i)
+        relayed = together(i, gath.at[far])
     if passed_on:
         pl.semaphore_wait(entry.at[0], 1)
         pl.semaphore_wait(entry.at[1], 1)
@@ -179,13 +200,11 @@
         block(y)
     for copy in local[5:]:
         copy.wait()
-    for copy in to_pas:
-        copy.wait_recv()
+    to_pas.wait_recv()
     for j in range(ny):
         pas_t[j] = pas[j].T
     if ny == 4:
-        for copy in relayed:
-            copy.wait_recv()
+        relayed.wait_recv()
         block(far)
     else:
         for d, copy in zip(y_far, direct):
@@ -216,28 +235,28 @@
     for j in range(NX):
         a, b = (j // 2) * tile, (j % 2) * 128
         sc_s[j] = score[a:a + tile, b:b + 128]
-    to_x = [remote(sc_s.at[around(x, d, NX)], sc_x.at[d], x_dev(d)) for d in x_far]
+    to_x = remotes([(sc_s.at[around(x, d, NX)], sc_x.at[d], x_dev(d)) for d in x_far], sc_x.at[pl.ds(1, NX - 1)])
     for j in range(ny):
         pos_s[j] = dot(onehot, pas[j]).astype(bf16)
-    to_pos = [remote(pos_s.at[around(y, d, ny)], pos_r.at[d], pass_dev(d, 0)) for d in y_far]
+    to_pos = remotes([(pos_s.at[around(y, d, ny)], pos_r.at[d], pass_dev(d, 0)) for d in y_far],
+                     pos_r.at[pl.ds(1, ny - 1)])
     to_wr = {}
     for d in y_far:
         rows = pl.ds(pl.multiple_of(around(y, d, ny) * chip_cols, chip_cols), chip_cols)
         to_wr[d] = remote(w_v.at[rows, mine], wr.at[y, :, mine], pass_dev(d, 0))
     for j in range(ny):
         sel_r[y, j * SLOT:(j + 1) * SLOT, :] = selp[j, 0:SLOT, :]
-    to_sel = [remote(sel_r.at[y], sel_r.at[y], pass_dev(d, 0)) for d in y_far]
+    to_sel = remotes([(sel_r.at[y], sel_r.at[y], pass_dev(d, 0)) for d in y_far], sel_r.at[pl.ds(0, ny - 1)])
     to_other = remote(gath, gath_o, sibling)
     total = sc_s[x]
-    for copy in to_x:
-        copy.wait_recv()
+    to_x.wait_recv()
     for d in range(1, NX):
         total = total + sc_x[d]
     zs[...] = total
     if passed_on:
         pl.semaphore_wait(entry.at[2], 1)
         pl.semaphore_wait(entry.at[3], 1)
-    to_z = [remote(zs, zr.at[d], z_dev(d)) for d in z_far]
+    to_z = remotes([(zs, zr.at[d], z_dev(d)) for d in z_far], zr.at[pl.ds(1, nz - 1)])
     wr_t[y] = w_v[pl.ds(pl.multiple_of(y * chip_cols, chip_cols), chip_cols), :].T
     prow = iota((tok, 128), 0)
     chunk = jnp.floor((prow.astype(f32) + 0.5) * (1.0 / ro)).astype(jnp.int32)
@@ -252,24 +271,22 @@
     at_sel = sela[...] + wide_bias
     slope[...] = jax.nn.sigmoid(at_sel) / (1.0 + jax.nn.softplus(at_sel))
     gath_t[0] = gath[...].reshape(tok, d_model).T
-    for copy in to_z:
-        copy.wait_recv()
+    to_z.wait_recv()
     for d in range(1, nz):
         total = total + zr[d]
     fin[x] = total
-    to_fin = [remote(fin.at[x], fin.at[x], x_dev(d)) for d in x_far]
-    to_wr_sib = []
+    to_fin = remotes([(fin.at[x], fin.at[x], x_dev(d)) for d in x_far], fin.at[pl.ds(0, NX - 1)])
+    i = take()
     for d in reversed(y_far):
         to_wr[d].wait_recv()
         there = around(y, -d, ny)
-        to_wr_sib.append(remote(wr.at[there, :, mine], wr.at[there, :, mine], sibling))
-    for copy in to_pos:
-        copy.wait_recv()
+        remote(wr.at[there, :, mine], wr.at[there, :, mine], sibling, i)
+    to_wr_sib = together(i, wr.at[pl.ds(0, ny - 1), :, mine])
+    to_pos.wait_recv()
     pos_entries = pos_s[y].astype(f32)
     for d in range(1, ny):
         pos_entries = pos_entries + pos_r[d].astype(f32)
-    for copy in to_fin:
-        copy.wait_recv()
+    to_fin.wait_recv()
 
     score = jnp.concatenate([jnp.concatenate([fin[j], fin[j + 1]], axis=1) for j in range(0, NX, 2)], axis=0)
     peak = jnp.max(score, axis=1, keepdims=True)
@@ -287,15 +304,14 @@
         there = around(y, d, ny)
         u_s[there] = dot(other, pas[there]).astype(bf16)
         to_u[d] = remote(u_s.at[there], u_r.at[d], pass_dev(d, 0))
-    to_st = [remote(st_s, st.at[d], pass_dev(d, 0)) for d in y_far]
+    to_st = remotes([(st_s, st.at[d], pass_dev(d, 0)) for d in y_far], st.at[pl.ds(1, ny - 1)])
     st[0] = st_s[...]
     mine_u = dot(other, pas[y])
-    for d, copy in zip(reversed(y_far), to_wr_sib):
-        copy.wait_recv()
+    to_wr_sib.wait_recv()
+    for d in y_far:
         there = around(y, -d, ny)
         wr_t[there] = wr[there].T
-    for copy in to_st:
-        copy.wait_recv()
+    to_st.wait_recv()
     peaks = [st[i][0:1] for i in range(ny)]
     highest = functools.reduce(jnp.maximum, peaks)
     scale = [jnp.exp(k - highest) for k in peaks]
@@ -332,8 +348,7 @@
     to_lh = remote(lh.at[:, theirs], lh_o, sibling)
 
     out = dot(lh[...], wr_t[y])
-    for copy in to_sel:
-        copy.wait_recv()
+    to_sel.wait_recv()
     for d in reversed(y_far):
         to_g[d].wait_recv()
         there = around(y, -d, ny)
@@ -343,8 +358,8 @@
     for k in range(NC):
         for j in range(NX):
             s1[k, j] = out[j * part:(j + 1) * part, k * 128:(k + 1) * 128]
-    to_s1 = [remote(s1.at[around(c, dc, NC), around(x, dx, NX)], s1_r.at[dx * NC + dc], x_dev(dx, dc))
-             for dx, dc in x_peers]
+    to_s1 = remotes([(s1.at[around(c, dc, NC), around(x, dx, NX)], s1_r.at[dx * NC + dc], x_dev(dx, dc))
+                     for dx, dc in x_peers], s1_r.at[pl.ds(1, NX * NC - 1)])
 
     at_row = iota((ROWS, wide), 0)
     real = (lax.bitwise_and(at_row, SLOT - 1) < per_block) & (at_row < ny * SLOT)
@@ -357,8 +372,7 @@
     gath_t[1] = gath_o[...].reshape(tok, d_model).T
     gw_v[...] = dot(gath_t[0], lh[:, mine])
 
-    for copy in to_s1:
-        copy.wait_recv()
+    to_s1.wait_recv()
     same, cross = s1[c, x].astype(f32), s1_r[1].astype(f32)
     for d in range(1, NX):
         same = same + s1_r[d * NC].astype(f32)
@@ -370,8 +384,8 @@
             to_row = (NC * (k // z_block) + core) * z_block + k % z_block
             zf[to_row, 0:ro, :] = high[core, k * ro:(k + 1) * ro]
     z2[...] = zf[...].astype(bf16)
-    to_z2 = [remote(z2.at[around(z, d, nz)], z2_r.at[d], z_dev(d)) for d in z_far]
-    for copy in started[:-len(to_z2)]:
+    to_z2 = remotes([(z2.at[around(z, d, nz)], z2_r.at[d], z_dev(d)) for d in z_far], z2_r.at[pl.ds(1, nz - 1)])
+    for copy in started[:-1]:
         copy.wait_send()
     to_lh.wait_recv()
     gw_v[...] += dot(gath_t[1], lh_o[...])
@@ -381,21 +395,22 @@
     gb_o[...] = (gs[c][0:1] + gs_r[0:1]).reshape(voc)
     loss_o[...] = (gs[c][1:2, 0:1] + gs_r[1:2, 0:1]) * (1.0 / n_queries)
     total = zf[z]
-    for copy in to_z2:
-        copy.wait_recv()
+    to_z2.wait_recv()
     for d in range(1, nz):
         total = total + z2_r[d].astype(f32)
     gh_o[...] = total[0:ro].astype(bf16)
 
-    for copy in to_z2:
-        copy.wait_send()
+    to_z2.wait_send()
     gw_out.wait()
 
 
 def hand_out(*refs):
     sems = refs[8]
-    copies = [pltpu.make_async_copy(refs[i], refs[4 + i], sems.at[i]) for i in range(4)]
-    for copy in copies:
+    pairs = [(refs[i], refs[4 + i]) for i in (0, 1, 3)]
+    rows = refs[2].shape[0] // 4
+    pairs += [(refs[2].at[pl.ds(i * rows, rows)], refs[6].at[pl.ds(i * rows, rows)]) for i in range(4)]
+    copies = [pltpu.make_async_copy(a, b, sems.at[i]) for i, (a, b) in enumerate(pairs)]
+    for copy in reversed(copies):
         copy.start()
     for copy in copies:
         copy.wait()
@@ -413,14 +428,13 @@
     tile = ROWS * 2 // NX
     i32 = jnp.int32
     vmem = pl.BlockSpec(memory_space=pltpu.VMEM)
-    smem = pl.BlockSpec(memory_space=pltpu.SMEM)
     anywhere = pl.BlockSpec(memory_space=pl.ANY)
     hbm = pl.BlockSpec(memory_space=pltpu.HBM)
     scratch = [
         ((ny, own_rows, d), bf16), ((ny, own_rows, d), bf16), ((NC, d, tok), bf16),
         ((d, wide), bf16), ((ny, NC * 128, wide), bf16), ((ny, wide, NC * 128), bf16),
         ((ny, NC * 128, wide), bf16), ((ny, wide, NC * 128), bf16), ((tok, tok), bf16),
-        ((voc,), f32), ((NC, 8, voc), f32), ((n_queries, qlen), i32), ((NC, n_queries, voc), i32),
+        ((voc,), f32), ((NC, 8, voc), f32), None, ((n_queries, qlen), i32), ((NC, n_queries, voc), i32),
         ((ny, 8, wide), i32), ((ny, 8, wide), i32),
         ((ny, 8, wide), f32), ((ny, 8, wide), f32), ((ROWS, wide), f32), ((ROWS, wide), f32),
         ((ny, ROWS, wide), bf16), ((ny, ROWS, wide), bf16), ((ny, ROWS, wide), bf16),
@@ -441,12 +455,12 @@
             jax.ShapeDtypeStruct((d, voc), f32),
             jax.ShapeDtypeStruct((voc,), f32),
         ),
-        in_specs=[hbm, hbm, hbm, hbm, hbm, smem, hbm],
+        in_specs=[hbm] * 7,
         out_specs=(vmem, vmem, anywhere, vmem),
-        scratch_shapes=[pltpu.VMEM(s, t) for s, t in scratch] + [
-            pltpu.SemaphoreType.DMA((MAX_COPIES,)),
-            pltpu.SemaphoreType.DMA((MAX_COPIES,)),
-            pltpu.SemaphoreType.DMA((5 + ny,)),
+        scratch_shapes=[pltpu.VMEM(*k) if k else pltpu.SMEM((n_queries,), i32) for k in scratch] + [
+            pltpu.SemaphoreType.DMA((MAX_SEMS,)),
+            pltpu.SemaphoreType.DMA((MAX_SEMS,)),
+            pltpu.SemaphoreType.DMA((6 + ny,)),
             pltpu.SemaphoreType.REGULAR((4,)),
         ],
         compiler_params=pltpu.CompilerParams(
@@ -459,7 +473,7 @@
         out_shape=tuple(jax.ShapeDtypeStruct(r.shape, r.dtype) for r in results),
         in_specs=[anywhere] * 4,
         out_specs=(hbm,) * 4,
-        scratch_shapes=[pltpu.SemaphoreType.DMA((4,))],
+        scratch_shapes=[pltpu.SemaphoreType.DMA((7,))],
         compiler_params=pltpu.CompilerParams(vmem_limit_bytes=1024 * 1024),
     )(*results)
     return loss.reshape(()), grad_hidden, grad_weight, grad_bias

time: 67 us -> 65 us (0.970)
  Pallas kernels: 66.2 us -> 64.2 us
    pallas_call x1, Pallas kernels: 64.4 us -> 62.4 us  [local(): pl.pallas_call(functools.partial(kernel, nz, ny, n_queries), out_shape=(j...]
where the time goes in v6:
time: 65 us; the launch traced here: 64.9 us
  Pallas kernels  64.2 us (99%)
    pallas_call x1, Pallas kernels, local(): pl.pallas_call(functools.partial(kernel, nz, ny, n_queries), out_shape=(j...  62.4 us
    pallas_call x1, Pallas kernels, local(): pl.pallas_call(hand_out, out_shape=tuple((jax.ShapeDtypeStruct(r.shape, r...  1.83 us

profile of v6, /device:TPU:1, one launch (start us, length us, event | category | flops | bytes accessed | tf_op | source)
XLA Modules:
  0.0 64.9 jit_solution(17503130061807400021)
XLA Ops:
  0.6 62.4 %shard_map.102 = (f32[1,1]{1,0:T(1,128)}, bf16[12,128]{1,0:T(8,128)(2,1)S(1)}, f32[1024,384]{1,0:T(8,128)S(1)}, f32[384]{0:T(512)S(1)}) custom-call(bf16[96,1024]{1,0:T(8,128)(2,1)} %hidden.1, bf16[1024,384]{1,0:T(8,128)(2,1)} %weight.1, f32[384]{0:T(512)} %bias.1, s32[24,32]{1,0:T(8,128)} %tokens.1, bf16[128,3072]{1,0:T(8,128)(2,1)} %passages.1, ...), custom_call_target="tpu_custom_call" | custom-call | tf_op jit(solution)/shard_map/pallas_call | solution.py:450
  63.0 1.8 %shard_map.103 = (f32[1,1]{1,0:T(1,128)}, bf16[12,128]{1,0:T(8,128)(2,1)}, f32[1024,384]{1,0:T(8,128)}, f32[384]{0:T(512)}) custom-call(f32[1,1]{1,0:T(1,128)} %get-tuple-element.12.refs_0_, bf16[12,128]{1,0:T(8,128)(2,1)S(1)} %get-tuple-element.13.refs_1_, f32[1024,384]{1,0:T(8,128)S(1)} %get-tuple-element.14.refs_2_, f32[384]{0:T(512)S(1)} %get-tuple-element.15.refs_3_), custom_call_target="tpu_custom_call" | custom-call | tf_op jit(solution)/shard_map/pallas_call | solution.py:471

commit v7 on v6

--- a/solution.py
+++ b/solution.py
@@ -12,7 +12,7 @@
 NC = 2
 SLOT = 4
 ROWS = 16
-MAX_SEMS = 37
+MAX_SEMS = 40
 MESH = pl.DeviceIdType.MESH
 f32 = jnp.float32
 bf16 = jnp.bfloat16
@@ -121,49 +121,59 @@
 
     barrier = pltpu.get_barrier_semaphore()
     passed_on = nz == 16
-    z_near = (2, -2, 1, -1) if passed_on else z_far
+    z_near = (1, -1) if passed_on else z_far
     peers = ([z_dev(d) for d in z_near] + [pass_dev(d, 0) for d in y_far] + [x_dev(*d) for d in x_peers])
     for device in peers:
         pl.semaphore_signal(barrier, inc=1, device_id=device, device_id_type=MESH)
     pl.semaphore_wait(barrier, len(peers))
 
-    hr = own_rows // 2
+    hr, hc = own_rows // 2, d_model // 2
     top, bottom = pl.ds(0, hr), pl.ds(hr, hr)
+    odd = lax.rem(x, 2)
+    kept = pl.ds(pl.multiple_of(odd * hc, 128), hc)
+    others = pl.ds(pl.multiple_of((1 - odd) * hc, 128), hc)
+
+    def to_plane(rows, dy):
+        return remote(hidden.at[rows, kept], gath.at[y, rows, kept], pass_dev(dy, 0))
+
+    def relay(yy, rows, dy, i):
+        remote(gath.at[yy, rows, kept], gath.at[yy, rows, kept], pass_dev(dy, 0), i)
+
+    def forward(yy, rows, dx, i):
+        remote(gath.at[yy, rows, kept], gath.at[yy, rows, kept], x_dev(dx), i)
+
     if ny == 4:
+        up, down, far = around(y, -1, ny), around(y, 1, ny), around(y, 2, ny)
         pieces = [(pl.ds(i, 16), pl.ds(hr + i, 16)) for i in range(0, hr, 16)]
-        first = []
-        for a, b in pieces:
-            first.append((remote(hidden.at[a], gath.at[y, a], pass_dev(1, 0)),
-                          remote(hidden.at[b], gath.at[y, b], pass_dev(-1, 0))))
-        then_up = remote(hidden.at[bottom], gath.at[y, bottom], pass_dev(1, 0))
-        then_down = remote(hidden.at[top], gath.at[y, top], pass_dev(-1, 0))
+        first = [(to_plane(a, 1), to_plane(b, -1)) for a, b in pieces]
+        then_up, then_down = to_plane(bottom, 1), to_plane(top, -1)
     else:
-        direct = [remote(hidden, gath.at[y], pass_dev(d, 0)) for d in y_far]
+        direct = [to_plane(pl.ds(0, own_rows), d) for d in y_far]
     if passed_on:
-        pl.semaphore_signal(entry.at[0], inc=1, device_id=z_dev(2), device_id_type=MESH)
-        pl.semaphore_signal(entry.at[1], inc=1, device_id=z_dev(-2), device_id_type=MESH)
+        pl.semaphore_signal(entry.at[0], inc=1, device_id=z_dev(1), device_id_type=MESH)
+        pl.semaphore_signal(entry.at[1], inc=1, device_id=z_dev(-1), device_id_type=MESH)
     to_w = remote(weight, w_v.at[:, mine], sibling)
+    if ny == 4:
+        i, i_up, i_down, i_far = take(), take(), take(), take()
+        for (a, b), (to_up, to_down) in zip(pieces, first):
+            to_up.wait_recv()
+            relay(up, a, 1, i)
+            to_down.wait_recv()
+            relay(down, b, -1, i)
+        relayed = together(i, gath.at[far, :, kept])
+        forward(up, top, 1, i_up)
+        forward(down, bottom, -1, i_down)
+    if passed_on:
+        pl.semaphore_wait(entry.at[0], 1)
+        pl.semaphore_wait(entry.at[1], 1)
+        pl.semaphore_signal(entry.at[2], inc=1, device_id=z_dev(2), device_id_type=MESH)
+        pl.semaphore_signal(entry.at[3], inc=1, device_id=z_dev(-2), device_id_type=MESH)
     for copy in local[:3]:
         copy.wait()
     bias_b[c] = jnp.broadcast_to(bias_v[...].reshape(1, voc), (8, voc))
     to_small = [remote(selected, sel_v.at[c], sibling), remote(bias_b.at[c], bias_b.at[c], sibling)]
     to_pas = remotes([(passages.at[:, pl.ds(j * wide, wide)], pas.at[j, mine_pas], sibling) for j in range(ny)],
                      pas.at[pl.ds(0, ny // 2)])
-
-    if ny == 4:
-        up, down, far = around(y, -1, ny), around(y, 1, ny), around(y, 2, ny)
-        i = take()
-        for (a, b), (to_up, to_down) in zip(pieces, first):
-            to_up.wait_recv()
-            remote(gath.at[up, a], gath.at[up, a], pass_dev(1, 0), i)
-            to_down.wait_recv()
-            remote(gath.at[down, b], gath.at[down, b], pass_dev(-1, 0), i)
-        relayed = together(i, gath.at[far])
-    if passed_on:
-        pl.semaphore_wait(entry.at[0], 1)
-        pl.semaphore_wait(entry.at[1], 1)
-        pl.semaphore_signal(entry.at[2], inc=1, device_id=z_dev(4), device_id_type=MESH)
-        pl.semaphore_signal(entry.at[3], inc=1, device_id=z_dev(-4), device_id_type=MESH)
     for ref in (maxl, sell, maxa, sela, selp, lenp, zf):
         ref[...] = jnp.zeros_like(ref)
 
@@ -186,30 +196,43 @@
         maxl[yy, 0:per_block, :] = jnp.max(jnp.where(valid, logits, -jnp.inf), axis=1)
         sell[yy, 0:per_block, :] = jnp.sum(jnp.where(chosen, logits, 0.0), axis=1)
 
+    if ny == 4:
+        then_up.wait_recv()
+        forward(up, bottom, -1, i_up)
+        from_x = [(up, together(i_up, gath.at[up, :, others]))]
+        then_down.wait_recv()
+        forward(down, top, 1, i_down)
+        from_x.append((down, together(i_down, gath.at[down, :, others])))
     local[3].wait()
     local[4].wait()
+    to_w.wait_recv()
+    block(y)
     if ny == 4:
-        to_w.wait_recv()
-        block(y)
-        then_up.wait_recv()
-        block(up)
-        then_down.wait_recv()
-        block(down)
+        relayed.wait_recv()
+        forward(far, top, 1, i_far)
+        forward(far, bottom, -1, i_far)
+        from_x.append((far, together(i_far, gath.at[far, :, others])))
     else:
-        to_w.wait_recv()
-        block(y)
+        from_x = []
+        for d, copy in zip(y_far, direct):
+            copy.wait_recv()
+            there, i = around(y, -d, ny), take()
+            forward(there, top, 1, i)
+            forward(there, bottom, -1, i)
+            from_x.append((there, together(i, gath.at[there, :, others])))
     for copy in local[5:]:
         copy.wait()
     to_pas.wait_recv()
     for j in range(ny):
         pas_t[j] = pas[j].T
-    if ny == 4:
-        relayed.wait_recv()
-        block(far)
-    else:
-        for d, copy in zip(y_far, direct):
-            copy.wait_recv()
-            block(around(y, -d, ny))
+    for n, (there, copy) in enumerate(from_x):
+        if n == 2 and passed_on:
+            pl.semaphore_wait(entry.at[2], 1)
+            pl.semaphore_wait(entry.at[3], 1)
+            pl.semaphore_signal(entry.at[4], inc=1, device_id=z_dev(4), device_id_type=MESH)
+            pl.semaphore_signal(entry.at[5], inc=1, device_id=z_dev(-4), device_id_type=MESH)
+        copy.wait_recv()
+        block(there)
 
     wide_bias = jnp.concatenate([bias_b[0], bias_b[1]], axis=1)[0:1]
     for j in range(ny):
@@ -254,8 +277,8 @@
         total = total + sc_x[d]
     zs[...] = total
     if passed_on:
-        pl.semaphore_wait(entry.at[2], 1)
-        pl.semaphore_wait(entry.at[3], 1)
+        pl.semaphore_wait(entry.at[4], 1)
+        pl.semaphore_wait(entry.at[5], 1)
     to_z = remotes([(zs, zr.at[d], z_dev(d)) for d in z_far], zr.at[pl.ds(1, nz - 1)])
     wr_t[y] = w_v[pl.ds(pl.multiple_of(y * chip_cols, chip_cols), chip_cols), :].T
     prow = iota((tok, 128), 0)
@@ -292,21 +315,21 @@
     peak = jnp.max(score, axis=1, keepdims=True)
     terms = jnp.exp(score - peak)
     other = jnp.where(is_pos, 0.0, terms)
+    half_other = other.astype(bf16)
+    to_u = {}
+    for d in y_far:
+        there = around(y, d, ny)
+        u_s[there] = dot(half_other, pas[there]).astype(bf16)
+        to_u[d] = remote(u_s.at[there], u_r.at[d], pass_dev(d, 0))
     stats = [peak, jnp.sum(other, axis=1, keepdims=True),
              jnp.sum(jnp.where(is_pos, terms, 0.0), axis=1, keepdims=True),
              jnp.sum(jnp.where(is_pos, score, 0.0), axis=1, keepdims=True)]
     eye = iota((ROWS, 128), 0) == iota((ROWS, 128), 1)
     turned = [jnp.sum(jnp.where(eye, s, 0.0), axis=0, keepdims=True) for s in stats]
     st_s[...] = jnp.concatenate(turned + [jnp.zeros((8 - len(turned), 128), f32)], axis=0)
-    other = other.astype(bf16)
-    to_u = {}
-    for d in y_far:
-        there = around(y, d, ny)
-        u_s[there] = dot(other, pas[there]).astype(bf16)
-        to_u[d] = remote(u_s.at[there], u_r.at[d], pass_dev(d, 0))
     to_st = remotes([(st_s, st.at[d], pass_dev(d, 0)) for d in y_far], st.at[pl.ds(1, ny - 1)])
     st[0] = st_s[...]
-    mine_u = dot(other, pas[y])
+    mine_u = dot(half_other, pas[y])
     to_wr_sib.wait_recv()
     for d in y_far:
         there = around(y, -d, ny)
@@ -461,7 +484,7 @@
             pltpu.SemaphoreType.DMA((MAX_SEMS,)),
             pltpu.SemaphoreType.DMA((MAX_SEMS,)),
             pltpu.SemaphoreType.DMA((6 + ny,)),
-            pltpu.SemaphoreType.REGULAR((4,)),
+            pltpu.SemaphoreType.REGULAR((6,)),
         ],
         compiler_params=pltpu.CompilerParams(
             collective_id=0, has_side_effects=True, vmem_limit_bytes=48 * 1024 * 1024

time: 65 us -> 66.2 us (1.018)
  Pallas kernels: 64.2 us -> 65.5 us
    pallas_call x1, Pallas kernels: 62.4 us -> 63.6 us  [local(): pl.pallas_call(functools.partial(kernel, nz, ny, n_queries), out_shape=(j...]
where the time goes in v7:
time: 66.2 us; the launch traced here: 66.1 us
  Pallas kernels  65.5 us (99%)
    pallas_call x1, Pallas kernels, local(): pl.pallas_call(functools.partial(kernel, nz, ny, n_queries), out_shape=(j...  63.6 us
    pallas_call x1, Pallas kernels, local(): pl.pallas_call(hand_out, out_shape=tuple((jax.ShapeDtypeStruct(r.shape, r...  1.83 us

profile of v7, /device:TPU:1, one launch (start us, length us, event | category | flops | bytes accessed | tf_op | source)
XLA Modules:
  0.0 66.1 jit_solution(7575987540817322223)
XLA Ops:
  0.6 63.6 %shard_map.102 = (f32[1,1]{1,0:T(1,128)}, bf16[12,128]{1,0:T(8,128)(2,1)S(1)}, f32[1024,384]{1,0:T(8,128)S(1)}, f32[384]{0:T(512)S(1)}) custom-call(bf16[96,1024]{1,0:T(8,128)(2,1)} %hidden.1, bf16[1024,384]{1,0:T(8,128)(2,1)} %weight.1, f32[384]{0:T(512)} %bias.1, s32[24,32]{1,0:T(8,128)} %tokens.1, bf16[128,3072]{1,0:T(8,128)(2,1)} %passages.1, ...), custom_call_target="tpu_custom_call" | custom-call | tf_op jit(solution)/shard_map/pallas_call | solution.py:473
  64.3 1.8 %shard_map.103 = (f32[1,1]{1,0:T(1,128)}, bf16[12,128]{1,0:T(8,128)(2,1)}, f32[1024,384]{1,0:T(8,128)}, f32[384]{0:T(512)}) custom-call(f32[1,1]{1,0:T(1,128)} %get-tuple-element.12.refs_0_, bf16[12,128]{1,0:T(8,128)(2,1)S(1)} %get-tuple-element.13.refs_1_, f32[1024,384]{1,0:T(8,128)S(1)} %get-tuple-element.14.refs_2_, f32[384]{0:T(512)S(1)} %get-tuple-element.15.refs_3_), custom_call_target="tpu_custom_call" | custom-call | tf_op jit(solution)/shard_map/pallas_call | solution.py:494

commit v8 on v6

--- a/solution.py
+++ b/solution.py
@@ -12,7 +12,7 @@
 NC = 2
 SLOT = 4
 ROWS = 16
-MAX_SEMS = 37
+MAX_SEMS = 35
 MESH = pl.DeviceIdType.MESH
 f32 = jnp.float32
 bf16 = jnp.bfloat16
@@ -33,7 +33,7 @@
 def kernel(nz, ny, n_queries, hidden, weight, bias, tokens, passages, positive_h, selected,
            loss_o, gh_o, gw_o, gb_o,
            gath, gath_o, gath_t, w_v, wr, wr_t, pas, pas_t, perm, bias_v, bias_b, positive, tokens_v, sel_v, selp, lenp,
-           maxl, sell, maxa, sela, pool, pos_s, pos_r, sc_s, sc_x, zs, zr, fin, st_s, st, u_s, u_r, slope,
+           maxl, sell, maxa, sela, pool, pos_s, pos_r, sc_s, sc_x, zs, zr, fin, st_s, st, u_s, u_r, slope, pos_f, grads,
            sel_r, g_r, lh, lh_y, lh_o, gs, gs_r, s1, s1_r, high,
            zf, z2, z2_r, gw_v, send_sems, recv_sems, loc_sems, entry):
     n_pass = ny * NC
@@ -238,7 +238,7 @@
     to_x = remotes([(sc_s.at[around(x, d, NX)], sc_x.at[d], x_dev(d)) for d in x_far], sc_x.at[pl.ds(1, NX - 1)])
     for j in range(ny):
         pos_s[j] = dot(onehot, pas[j]).astype(bf16)
-    to_pos = remotes([(pos_s.at[around(y, d, ny)], pos_r.at[d], pass_dev(d, 0)) for d in y_far],
+    to_pos = remotes([(pos_s, pos_r.at[d], pass_dev(d, 0)) for d in y_far],
                      pos_r.at[pl.ds(1, ny - 1)])
     to_wr = {}
     for d in y_far:
@@ -269,7 +269,8 @@
     for j in range(ny):
         sela[j * SLOT:(j + 1) * SLOT, :] = sell[j, 0:SLOT, :]
     at_sel = sela[...] + wide_bias
-    slope[...] = jax.nn.sigmoid(at_sel) / (1.0 + jax.nn.softplus(at_sel))
+    slope[y] = jax.nn.sigmoid(at_sel) / (1.0 + jax.nn.softplus(at_sel))
+    to_slope = remotes([(slope.at[y], slope.at[y], pass_dev(d, 0)) for d in y_far], slope.at[pl.ds(0, ny - 1)])
     gath_t[0] = gath[...].reshape(tok, d_model).T
     to_z.wait_recv()
     for d in range(1, nz):
@@ -283,9 +284,11 @@
         remote(wr.at[there, :, mine], wr.at[there, :, mine], sibling, i)
     to_wr_sib = together(i, wr.at[pl.ds(0, ny - 1), :, mine])
     to_pos.wait_recv()
-    pos_entries = pos_s[y].astype(f32)
-    for d in range(1, ny):
-        pos_entries = pos_entries + pos_r[d].astype(f32)
+    for j in range(ny):
+        entries = pos_s[j].astype(f32)
+        for d in range(1, ny):
+            entries = entries + pos_r[d, j].astype(f32)
+        pos_f[j] = entries
     to_fin.wait_recv()
 
     score = jnp.concatenate([jnp.concatenate([fin[j], fin[j + 1]], axis=1) for j in range(0, NX, 2)], axis=0)
@@ -299,14 +302,11 @@
     turned = [jnp.sum(jnp.where(eye, s, 0.0), axis=0, keepdims=True) for s in stats]
     st_s[...] = jnp.concatenate(turned + [jnp.zeros((8 - len(turned), 128), f32)], axis=0)
     other = other.astype(bf16)
-    to_u = {}
-    for d in y_far:
-        there = around(y, d, ny)
-        u_s[there] = dot(other, pas[there]).astype(bf16)
-        to_u[d] = remote(u_s.at[there], u_r.at[d], pass_dev(d, 0))
+    for j in range(ny):
+        u_s[j] = dot(other, pas[j]).astype(bf16)
+    to_u = {d: remote(u_s, u_r.at[d], pass_dev(d, 0)) for d in y_far}
     to_st = remotes([(st_s, st.at[d], pass_dev(d, 0)) for d in y_far], st.at[pl.ds(1, ny - 1)])
     st[0] = st_s[...]
-    mine_u = dot(other, pas[y])
     to_wr_sib.wait_recv()
     for d in y_far:
         there = around(y, -d, ny)
@@ -327,14 +327,19 @@
     def column(line):
         return jnp.sum(jnp.where(eye, line, 0.0), axis=1, keepdims=True)
 
-    term = column(scale[0] * factor) * mine_u - column(rest * factor) * pos_entries
+    weights, pos_weight = [column(k * factor) for k in scale], column(rest * factor)
+    for j in range(ny):
+        grads[j] = weights[0] * u_s[j].astype(f32) - pos_weight * pos_f[j]
+    to_slope.wait_recv()
     for d in reversed(y_far):
         to_u[d].wait_recv()
-        term = term + column(scale[d] * factor) * u_r[d].astype(f32)
-
-    grad = term * slope[...]
-    g_r[y] = grad.astype(bf16)
-    to_g = {d: remote(g_r.at[y], g_r.at[y], pass_dev(d, 0)) for d in y_far}
+        for j in range(ny):
+            grads[j] += weights[d] * u_r[d, j].astype(f32)
+
+    for j in range(ny):
+        grads[j] = grads[j] * slope[j]
+        g_r[j] = grads[j].astype(bf16)
+    grad = grads[y]
     at = iota((per_block, qlen, wide), 1)
 
     def spread(yy, out):
@@ -350,7 +355,6 @@
     out = dot(lh[...], wr_t[y])
     to_sel.wait_recv()
     for d in reversed(y_far):
-        to_g[d].wait_recv()
         there = around(y, -d, ny)
         spread(there, lh_y)
         out = out + dot(lh_y[...], wr_t[there])
@@ -437,10 +441,11 @@
         ((voc,), f32), ((NC, 8, voc), f32), None, ((n_queries, qlen), i32), ((NC, n_queries, voc), i32),
         ((ny, 8, wide), i32), ((ny, 8, wide), i32),
         ((ny, 8, wide), f32), ((ny, 8, wide), f32), ((ROWS, wide), f32), ((ROWS, wide), f32),
-        ((ny, ROWS, wide), bf16), ((ny, ROWS, wide), bf16), ((ny, ROWS, wide), bf16),
+        ((ny, ROWS, wide), bf16), ((ny, ROWS, wide), bf16), ((ny, ny, ROWS, wide), bf16),
         ((NX, tile, 128), f32), ((NX, tile, 128), f32), ((tile, 128), f32), ((nz, tile, 128), f32),
         ((NX, tile, 128), f32), ((8, 128), f32), ((ny, 8, 128), f32),
-        ((ny, ROWS, wide), bf16), ((ny, ROWS, wide), bf16), ((ROWS, wide), f32),
+        ((ny, ROWS, wide), bf16), ((ny, ny, ROWS, wide), bf16), ((ny, ROWS, wide), f32),
+        ((ny, ROWS, wide), f32), ((ny, ROWS, wide), f32),
         ((ny, ROWS, wide), i32), ((ny, ROWS, wide), bf16),
         ((tok, wide), bf16), ((tok, wide), bf16), ((tok, voc), bf16),
         ((NC, 8, voc), f32), ((8, voc), f32),

time: 65 us -> 67.2 us (1.034)
  Pallas kernels: 64.2 us -> 66.5 us
    pallas_call x1, Pallas kernels: 62.4 us -> 64.6 us  [local(): pl.pallas_call(functools.partial(kernel, nz, ny, n_queries), out_shape=(j...]
where the time goes in v8:
time: 67.2 us; the launch traced here: 67.1 us
  Pallas kernels  66.5 us (99%)
    pallas_call x1, Pallas kernels, local(): pl.pallas_call(functools.partial(kernel, nz, ny, n_queries), out_shape=(j...  64.6 us
    pallas_call x1, Pallas kernels, local(): pl.pallas_call(hand_out, out_shape=tuple((jax.ShapeDtypeStruct(r.shape, r...  1.83 us

profile of v8, /device:TPU:1, one launch (start us, length us, event | category | flops | bytes accessed | tf_op | source)
XLA Modules:
  0.0 67.1 jit_solution(13000114432032639426)
XLA Ops:
  0.6 64.6 %shard_map.102 = (f32[1,1]{1,0:T(1,128)}, bf16[12,128]{1,0:T(8,128)(2,1)S(1)}, f32[1024,384]{1,0:T(8,128)S(1)}, f32[384]{0:T(512)S(1)}) custom-call(bf16[96,1024]{1,0:T(8,128)(2,1)} %hidden.1, bf16[1024,384]{1,0:T(8,128)(2,1)} %weight.1, f32[384]{0:T(512)} %bias.1, s32[24,32]{1,0:T(8,128)} %tokens.1, bf16[128,3072]{1,0:T(8,128)(2,1)} %passages.1, ...), custom_call_target="tpu_custom_call" | custom-call | tf_op jit(solution)/shard_map/pallas_call | solution.py:455
  65.3 1.8 %shard_map.103 = (f32[1,1]{1,0:T(1,128)}, bf16[12,128]{1,0:T(8,128)(2,1)}, f32[1024,384]{1,0:T(8,128)}, f32[384]{0:T(512)}) custom-call(f32[1,1]{1,0:T(1,128)} %get-tuple-element.12.refs_0_, bf16[12,128]{1,0:T(8,128)(2,1)S(1)} %get-tuple-element.13.refs_1_, f32[1024,384]{1,0:T(8,128)S(1)} %get-tuple-element.14.refs_2_, f32[384]{0:T(512)S(1)} %get-tuple-element.15.refs_3_), custom_call_target="tpu_custom_call" | custom-call | tf_op jit(solution)/shard_map/pallas_call | solution.py:476

commit v9 on v6

--- a/solution.py
+++ b/solution.py
@@ -198,11 +198,6 @@
     else:
         to_w.wait_recv()
         block(y)
-    for copy in local[5:]:
-        copy.wait()
-    to_pas.wait_recv()
-    for j in range(ny):
-        pas_t[j] = pas[j].T
     if ny == 4:
         relayed.wait_recv()
         block(far)
@@ -216,6 +211,11 @@
         maxa[j * SLOT:(j + 1) * SLOT, :] = maxl[j, 0:SLOT, :]
     pool[y] = jnp.log1p(jax.nn.softplus(maxa[...] + wide_bias)).astype(bf16)
     to_pool = {d: remote(pool.at[y], pool.at[y], pass_dev(d, 0)) for d in y_far}
+    for copy in local[5:]:
+        copy.wait()
+    to_pas.wait_recv()
+    for j in range(ny):
+        pas_t[j] = pas[j].T
     row, lane = iota((ROWS, 256), 0), iota((ROWS, 256), 1)
     place = lax.bitwise_and(row, SLOT - 1)
     query = (lax.shift_right_logical(row, 2) * NC + c) * per_block + place

time: 65 us -> 65 us (level)
  no operation moved by 1% of the time
where the time goes in v9:
time: 65 us; the launch traced here: 64.8 us
  Pallas kernels  64.2 us (99%)
    pallas_call x1, Pallas kernels, local(): pl.pallas_call(functools.partial(kernel, nz, ny, n_queries), out_shape=(j...  62.4 us
    pallas_call x1, Pallas kernels, local(): pl.pallas_call(hand_out, out_shape=tuple((jax.ShapeDtypeStruct(r.shape, r...  1.83 us

profile of v9, /device:TPU:1, one launch (start us, length us, event | category | flops | bytes accessed | tf_op | source)
XLA Modules:
  0.0 64.8 jit_solution(8525943489221513792)
XLA Ops:
  0.6 62.4 %shard_map.102 = (f32[1,1]{1,0:T(1,128)}, bf16[12,128]{1,0:T(8,128)(2,1)S(1)}, f32[1024,384]{1,0:T(8,128)S(1)}, f32[384]{0:T(512)S(1)}) custom-call(bf16[96,1024]{1,0:T(8,128)(2,1)} %hidden.1, bf16[1024,384]{1,0:T(8,128)(2,1)} %weight.1, f32[384]{0:T(512)} %bias.1, s32[24,32]{1,0:T(8,128)} %tokens.1, bf16[128,3072]{1,0:T(8,128)(2,1)} %passages.1, ...), custom_call_target="tpu_custom_call" | custom-call | tf_op jit(solution)/shard_map/pallas_call | solution.py:450
  63.0 1.8 %shard_map.103 = (f32[1,1]{1,0:T(1,128)}, bf16[12,128]{1,0:T(8,128)(2,1)}, f32[1024,384]{1,0:T(8,128)}, f32[384]{0:T(512)}) custom-call(f32[1,1]{1,0:T(1,128)} %get-tuple-element.12.refs_0_, bf16[12,128]{1,0:T(8,128)(2,1)S(1)} %get-tuple-element.13.refs_1_, f32[1024,384]{1,0:T(8,128)S(1)} %get-tuple-element.14.refs_2_, f32[384]{0:T(512)S(1)} %get-tuple-element.15.refs_3_), custom_call_target="tpu_custom_call" | custom-call | tf_op jit(solution)/shard_map/pallas_call | solution.py:471
